TPU v7x, 32 devices: a whole 2x2x4 slice. The times are simulated.
32 devices in a mesh: slides: 2 (over x), seq: 16 (over z, y, core).
Axes of the slice: x: 2, y: 2, z: 4, core: 2. Of those that a mesh axis runs over, the one named last changes fastest.
Arguments:
- queries: bfloat16 [16384, 768], P(('slides', 'seq')), parts along dimension 0, may hold values from -72 to 72
- key_rows: bfloat16 [16384, 768], P(('slides', 'seq')), parts along dimension 0, may hold values from -6 to 6
- value_rows: bfloat16 [16384, 768], P(('slides', 'seq')), parts along dimension 0, may hold values from -6 to 6
- offsets: int32 [3, 16], replicated, may hold values from 0 to 15, as said below
Outputs:
- attended: bfloat16 [16384, 768], P(('slides', 'seq')), parts along dimension 0
There are 2 independent parts, one for each index of `slides`. A program takes and returns all parts, laid end to end along the dimension named above; an argument that names none is the same for every part. Nothing has to cross between parts.
Inputs may be any that keep to these rules, and one draw needn't show every extreme that they name: offsets[0, h] is below 4, offsets[1, h] below 16, offsets[2, h] below 16; some head has offset 16 - 1 at the widest scale.
All inputs are finite; a program needn't handle non-finite values.
Results may differ from a plain program's by a relative error of at most 0.0045.
Values may be sent and summed in bfloat16 or wider, within the bound.
No kernel may reach another device: no remote copies, remote signals or barrier semaphores. Data moves between devices by JAX's collectives and lax.ppermute only.
A program may use at most 128 MiB of HBM per device.

v0:
```python
import functools

import jax
import jax.numpy as jnp
from jax import lax
from jax.experimental import pallas as pl
from jax.experimental.pallas import tpu as pltpu
from jax.sharding import PartitionSpec as P

H = 16
HD = 48
D = 768
NEAR_SPAN = 4
MID_SPAN = 16
HALF = 384
TILE = 128
HALF_HEADS = HALF // HD
PARTS = D // HALF
PART_TILES = HALF // TILE
STAT_LANE = (2 * HD, 2 * HD + 16)
SCALE = HD ** (-0.5)
LOG2E = 1.4426950408889634
VMEM_BYTES = 63 * 1024 * 1024
SMALL_BYTES = 48 * 1024 * 1024
OWNED_BYTES = 32 * 1024 * 1024
BF = jnp.bfloat16
F32 = jnp.float32


def from_partner(block, axis, flip):
    count = lax.axis_size(axis)
    return lax.ppermute(block, axis, [(i, i ^ flip) for i in range(count)])


def params(limit=VMEM_BYTES):
    return pltpu.CompilerParams(vmem_limit_bytes=limit)


def cost(flops, moved, exps=0):
    return pl.CostEstimate(flops=flops, bytes_accessed=moved, transcendentals=exps)


def tile_offsets(offsets_ref, scale, tile, rows):
    lane = lax.broadcasted_iota(jnp.int32, (rows, TILE), 1)
    heads = list(heads_of(tile))
    result = jnp.full((rows, TILE), offsets_ref[scale, heads[0]], jnp.int32)
    for h in heads[1:]:
        result = jnp.where(lane >= h * HD - tile * TILE, offsets_ref[scale, h], result)
    return result


def inside(lane, low, high):
    return jnp.where((lane >= low) & (lane < high), F32(1.0), F32(0.0)).astype(BF)


def heads_of(tile):
    return range(tile * TILE // HD, ((tile + 1) * TILE - 1) // HD + 1)


def tiles_of(head):
    return range(head * HD // TILE, ((head + 1) * HD - 1) // TILE + 1)


def every(first, rows):
    return pl.ds(first, rows // MID_SPAN, stride=MID_SPAN)


def bits_of(offs, count):
    return [(offs & (1 << k)) != 0 for k in range(count.bit_length() - 1)]


def pick(blocks, bits):
    for bit in bits:
        blocks = [jnp.where(bit, high, low) for low, high in zip(blocks[::2], blocks[1::2])]
    return blocks[0]


def lanes_of(part):
    return slice(part * HALF, (part + 1) * HALF)


def flights(pairs, sems):
    copies = [pltpu.make_async_copy(src, dst, sems.at[i]) for i, (src, dst) in enumerate(pairs)]
    for copy in copies:
        copy.start()
    return copies


def scale_lane(scale):
    return scale * HD


def prep_kernel(
    wide, offsets_ref, q_ref, k_ref, v_ref, near_q_out, near_out, send_out,
    stage, single, near_q, near, send, in_sems, out_sems,
):
    rows = q_ref.shape[0]
    groups = rows // MID_SPAN
    near_rows = rows // NEAR_SPAN
    arrivals = flights(
        [
            (ref.at[:, lanes_of(part)], stage.at[x, :, lanes_of(part)])
            for part in range(PARTS)
            for x, ref in enumerate((q_ref, k_ref, v_ref))
        ],
        in_sems,
    )
    lane = lax.broadcasted_iota(jnp.int32, (groups, TILE), 1)
    leaving = []
    for part in range(PARTS):
        here = lanes_of(part)
        tiles = range(part * PART_TILES, (part + 1) * PART_TILES)
        bits = [
            {t: bits_of(tile_offsets(offsets_ref, s, t, groups), MID_SPAN if s else NEAR_SPAN) for t in tiles}
            for s in range(1 + wide)
        ]
        for x in range(3):
            arrivals[part * 3 + x].wait()
            chosen = [{} for _ in range(wide)]
            for t in tiles:
                lanes = slice(t * TILE, (t + 1) * TILE)
                single[x, t] = stage[x, :, lanes].astype(F32)
                block = [single[x, t, every(o, rows), :] for o in range(MID_SPAN)]
                for a in range(NEAR_SPAN):
                    picked = pick(block[a * NEAR_SPAN : (a + 1) * NEAR_SPAN], bits[0][t]).astype(BF)
                    if x == 0:
                        near_q[a * groups : (a + 1) * groups, lanes] = picked
                    else:
                        base = (x - 1) * near_rows + a * groups
                        near[base : base + groups, lanes] = picked
                for s in range(wide):
                    picked = pick(block, bits[1 + s][t])
                    chosen[s][t] = pltpu.roll(picked, scale_lane(s), 1) if s else picked
            for h in range(part * HALF_HEADS, (part + 1) * HALF_HEADS):
                travel = jnp.zeros((groups, TILE), F32)
                for s in range(wide):
                    for t in tiles_of(h):
                        low, high = max(h * HD, t * TILE), min((h + 1) * HD, (t + 1) * TILE)
                        turned = (lane - scale_lane(s)) & (TILE - 1)
                        hit = (turned >= low - t * TILE) & (turned < high - t * TILE)
                        travel = jnp.where(hit, chosen[s][t], travel)
                send[h * 3 * groups + x * groups : h * 3 * groups + (x + 1) * groups, :] = travel.astype(BF)
        owners = slice(part * HALF_HEADS * 3 * groups, (part + 1) * HALF_HEADS * 3 * groups)
        leaving += flights(
            [
                (send.at[owners], send_out.at[owners]),
                (near.at[:, here], near_out.at[:, here]),
                (near_q.at[:, here], near_q_out.at[:, here]),
            ],
            out_sems.at[part],
        )
    for copy in leaving:
        copy.wait()


def probabilities(scores):
    top = jnp.max(scores, axis=1, keepdims=True)
    return jnp.exp2((scores - top) * F32(SCALE * LOG2E)).astype(BF), top


def attend_half(q, k, v, stacked):
    count = q.shape[0]
    lane = lax.broadcasted_iota(jnp.int32, (1, TILE), 1)
    full_lane = lax.broadcasted_iota(jnp.int32, (count, TILE), 1)
    wide_lane = lax.broadcasted_iota(jnp.int32, (1, 2 * TILE), 1)
    num = [None] * 3
    den = [None] * 3
    top_tiles = [jnp.zeros((count, TILE), F32) for _ in range(3)]

    def add(into, tile, value):
        into[tile] = value if into[tile] is None else into[tile] + value

    def masked_query(h, start):
        return q[:, start : start + 2 * TILE] * inside(wide_lane, h * HD - start, (h + 1) * HD - start)

    def scores_of(left, start):
        right = k[:, start : start + 2 * TILE]
        return lax.dot_general(left, right, (((1,), (1,)), ((), ())), preferred_element_type=F32)

    starts = [0 if (h + 1) * HD <= 2 * TILE else TILE for h in range(HALF_HEADS)]
    ready = {}
    if stacked:
        for start in (0, TILE):
            members = [h for h in range(HALF_HEADS) if starts[h] == start]
            together = scores_of(jnp.concatenate([masked_query(h, start) for h in members], axis=0), start)
            for i, h in enumerate(members):
                ready[h] = together[i * count : (i + 1) * count]
    for h in range(HALF_HEADS):
        low, high = h * HD, (h + 1) * HD
        scores = ready[h] if stacked else scores_of(masked_query(h, starts[h]), starts[h])
        probs, top = probabilities(scores)
        first, last = low // TILE, (high - 1) // TILE
        inside_first = (full_lane >= low - first * TILE) & (full_lane < high - first * TILE)
        ones_first = inside(lane, low - first * TILE, high - first * TILE)
        v_first = v[:, first * TILE : (first + 1) * TILE] * ones_first
        if first == last:
            weights = jnp.concatenate([v_first, jnp.broadcast_to(ones_first, v_first.shape)], axis=1)
            result = jnp.dot(probs, weights, preferred_element_type=F32)
            add(num, first, result[:, :TILE])
            add(den, first, result[:, TILE:])
            top_tiles[first] = jnp.where(inside_first, top, top_tiles[first])
        else:
            inside_last = full_lane < high - last * TILE
            ones_last = inside(lane, 0, high - last * TILE)
            v_last = v[:, last * TILE : (last + 1) * TILE] * ones_last
            weights = jnp.concatenate([v_first + ones_last, v_last + ones_first], axis=1)
            result = jnp.dot(probs, weights, preferred_element_type=F32)
            left, right = result[:, :TILE], result[:, TILE:]
            zero = F32(0.0)
            add(num, first, jnp.where(inside_first, left, zero))
            add(den, first, jnp.where(inside_first, right, zero))
            add(num, last, jnp.where(inside_last, right, zero))
            add(den, last, jnp.where(inside_last, left, zero))
            top_tiles[first] = jnp.where(inside_first, top, top_tiles[first])
            top_tiles[last] = jnp.where(inside_last, top, top_tiles[last])
    branch = [n / d for n, d in zip(num, den)]
    lse = [t * F32(SCALE) + jnp.log(d) for t, d in zip(top_tiles, den)]
    return branch, lse


def local_kernel(q_ref, k_ref, v_ref, own_out, stage, own, in_sems, out_sems):
    arrivals = flights(
        [
            (ref.at[:, lanes_of(part)], stage.at[x, :, lanes_of(part)])
            for part in range(PARTS)
            for x, ref in enumerate((q_ref, k_ref, v_ref))
        ],
        in_sems,
    )
    leaving = []
    for part in range(PARTS):
        here = lanes_of(part)
        for x in range(3):
            arrivals[part * 3 + x].wait()
        branch_tiles, lse_tiles = attend_half(stage[0, :, here], stage[1, :, here], stage[2, :, here], False)
        for t in range(PART_TILES):
            own[0, part * PART_TILES + t] = branch_tiles[t]
            own[1, part * PART_TILES + t] = lse_tiles[t]
        tiles = range(part * PART_TILES, (part + 1) * PART_TILES)
        leaving += flights([(own.at[i, t], own_out.at[i, t]) for i in range(2) for t in tiles], out_sems.at[part])
    for copy in leaving:
        copy.wait()


def combine(branch_a, lse_a, branch_b, lse_b):
    high = jnp.maximum(lse_a, lse_b)
    weight_a = jnp.exp(lse_a - high)
    weight_b = jnp.exp(lse_b - high)
    total = weight_a + weight_b
    return (weight_a * branch_a + weight_b * branch_b) / total, high + jnp.log(total)


def near_kernel(wide, offsets_ref, q_ref, *refs):
    kv_refs, (own_ref, state_out) = refs[:NEAR_SPAN], refs[NEAR_SPAN : NEAR_SPAN + 2]
    q_stage, kv_stage, own, picked, kv_sems, own_sems, out_sems = refs[NEAR_SPAN + 2 :]
    near_rows = q_ref.shape[0]
    rows = own_ref.shape[2]
    groups = rows // MID_SPAN
    arrivals, own_arrivals, leaving = [], [], []
    for part in range(PARTS):
        here = lanes_of(part)
        pairs = [(q_ref.at[:, here], q_stage.at[:, here])]
        for i, ref in enumerate(kv_refs):
            for x in range(2):
                rows_x = slice(x * near_rows, (x + 1) * near_rows)
                rows_i = slice(i * near_rows, (i + 1) * near_rows)
                pairs.append((ref.at[rows_x, here], kv_stage.at[x, rows_i, here]))
        arrivals.append(flights(pairs, kv_sems.at[part]))
        tiles = range(part * PART_TILES, (part + 1) * PART_TILES)
        own_arrivals.append(
            flights([(own_ref.at[i, t], own.at[i, t]) for i in range(2) for t in tiles], own_sems.at[part])
        )
    for part in range(PARTS):
        here = lanes_of(part)
        for copy in arrivals[part]:
            copy.wait()
        near_branch, near_lse = attend_half(q_stage[:, here], kv_stage[0, :, here], kv_stage[1, :, here], True)
        for copy in own_arrivals[part]:
            copy.wait()
        for i in range(PART_TILES):
            t = part * PART_TILES + i
            branch = [own[0, t, every(o, rows), :] for o in range(MID_SPAN)]
            lse = [own[1, t, every(o, rows), :] for o in range(MID_SPAN)]
            offs = tile_offsets(offsets_ref, 0, t, groups)
            hits, bits = [offs == b for b in range(NEAR_SPAN)], bits_of(offs, NEAR_SPAN)
            for a in range(NEAR_SPAN):
                members = slice(a * NEAR_SPAN, (a + 1) * NEAR_SPAN)
                span = slice(a * groups, (a + 1) * groups)
                mixed, high = combine(
                    pick(branch[members], bits), pick(lse[members], bits), near_branch[i][span], near_lse[i][span]
                )
                for b, hit in enumerate(hits):
                    o = a * NEAR_SPAN + b
                    branch[o] = jnp.where(hit, mixed, branch[o])
                    lse[o] = jnp.where(hit, high, lse[o])
            for o in range(MID_SPAN):
                own[0, t, every(o, rows), :] = branch[o]
            for s in range(wide):
                bits = bits_of(tile_offsets(offsets_ref, 1 + s, t, groups), MID_SPAN)
                for kind, blocks in enumerate((branch, lse)):
                    base = (2 * s + kind) * groups
                    picked[t, base : base + groups] = pick(blocks, bits)
        tiles = range(part * PART_TILES, (part + 1) * PART_TILES)
        pairs = [(own.at[0, t], state_out.at[t]) for t in tiles]
        pairs += [(picked.at[t], state_out.at[D // TILE + t, : 2 * wide * groups]) for t in tiles]
        leaving += flights(pairs, out_sems.at[part])
    for copy in leaving:
        copy.wait()


def owned_kernel(wide, recv_ref, back_out, back, out_sems):
    groups = recv_ref.shape[0] // (3 * MID_SPAN)
    head = lax.rem(lax.axis_index("seq"), H)
    lane = lax.broadcasted_iota(jnp.int32, (1, TILE), 1)
    row_place = (lane - head * HD) & (TILE - 1)

    def rows_of(x):
        starts = [(3 * peer + x) * groups for peer in range(MID_SPAN)]
        return jnp.concatenate([recv_ref[start : start + groups, :] for start in starts], axis=0)

    q, k, v = (rows_of(x) for x in range(3))
    full_lane = lax.broadcasted_iota(jnp.int32, (q.shape[0], TILE), 1)
    place = (full_lane - head * HD) & (TILE - 1)
    num_den = None
    tops = jnp.zeros((q.shape[0], TILE), F32)
    for s in range(wide):
        low = scale_lane(s)
        columns = inside(row_place, low, low + HD)
        totals = columns + inside(row_place, STAT_LANE[s], STAT_LANE[s] + 3)
        scores = lax.dot_general(q * columns, k, (((1,), (1,)), ((), ())), preferred_element_type=F32)
        probs, top = probabilities(scores)
        weights = jnp.concatenate([v * columns, jnp.broadcast_to(totals, v.shape)], axis=1)
        result = jnp.dot(probs, weights, preferred_element_type=F32)
        num_den = result if num_den is None else num_den + result
        tops = jnp.where((place >= STAT_LANE[s]) & (place < STAT_LANE[s] + 3), top, tops)
    den = num_den[:, TILE:]
    used = den > F32(0.0)
    den = jnp.where(used, den, F32(1.0))
    branch = num_den[:, :TILE] / den
    lse = tops * F32(SCALE) + jnp.log(den)
    first = lse.astype(BF).astype(F32)
    second = (lse - first).astype(BF).astype(F32)
    third = lse - first - second
    stat = place
    for s in range(wide):
        stat = jnp.where(place >= STAT_LANE[s], place - STAT_LANE[s], stat)
    split = jnp.where(stat == 0, first, jnp.where(stat == 1, second, third))
    split = jnp.where(used, split, F32(0.0))
    back[...] = jnp.where(place < wide * HD, branch, split).astype(BF)
    for copy in flights([(back, back_out)], out_sems):
        copy.wait()


def merge_kernel(wide, offsets_ref, back_ref, state_ref, out_ref, base, picked, out, in_sems, out_sems):
    rows = out_ref.shape[0]
    groups = rows // MID_SPAN
    arrivals = []
    for part in range(PARTS):
        tiles = range(part * PART_TILES, (part + 1) * PART_TILES)
        pairs = [(state_ref.at[D // TILE + t, : 2 * wide * groups], picked.at[t]) for t in tiles]
        pairs += [(state_ref.at[t], base.at[t]) for t in tiles]
        arrivals.append(flights(pairs, in_sems.at[part]))
    lane = lax.broadcasted_iota(jnp.int32, (1, TILE), 1)
    full_lane = lax.broadcasted_iota(jnp.int32, (groups, TILE), 1)
    ones = jnp.ones((TILE, TILE), BF)
    branches, lses = [], []
    for s in range(wide):
        turned, stats = [], []
        for h in range(H):
            mine = back_ref[h * groups : (h + 1) * groups, :]
            place = (lane - h * HD) & (TILE - 1)
            stats.append(mine * inside(place, STAT_LANE[s], STAT_LANE[s] + 3))
            single = mine.astype(F32)
            turned.append(pltpu.roll(single, TILE - scale_lane(s), 1) if s else single)
        branches.append(turned)
        lses.append(jnp.dot(jnp.concatenate(stats, axis=0), ones, preferred_element_type=F32))

    def by_tile(t, of_head):
        heads = list(heads_of(t))
        result = of_head(heads[0])
        for h in heads[1:]:
            result = jnp.where(full_lane >= h * HD - t * TILE, of_head(h), result)
        return result

    leaving = []
    for part in range(PARTS):
        here = lanes_of(part)
        for copy in arrivals[part]:
            copy.wait()
        for t in range(part * PART_TILES, (part + 1) * PART_TILES):
            offs, results = [], []
            for s in range(wide):
                start = 2 * s * groups
                branch, lse = picked[t, start : start + groups], picked[t, start + groups : start + 2 * groups]
                offs.append(tile_offsets(offsets_ref, 1 + s, t, groups))
                for before, (other_branch, other_lse) in zip(offs, results):
                    branch = jnp.where(before == offs[s], other_branch, branch)
                    lse = jnp.where(before == offs[s], other_lse, lse)
                wide_branch = by_tile(t, lambda h: branches[s][h])
                wide_lse = by_tile(t, lambda h: lses[s][h * groups : (h + 1) * groups])
                results.append(combine(branch, lse, wide_branch, wide_lse))
            for o in range(MID_SPAN):
                block = base[t, every(o, rows), :]
                for off, (branch, _) in zip(offs, results):
                    block = jnp.where(off == o, branch, block)
                base[t, every(o, rows), :] = block
            out[:, t * TILE : (t + 1) * TILE] = base[t].astype(BF)
        leaving += flights([(out.at[:, here], out_ref.at[:, here])], out_sems.at[part])
    for copy in leaving:
        copy.wait()


def far_by_gather(queries, key_rows, value_rows, choose, dilation):
    rows = queries.shape[0]

    def select(data):
        shaped = data.reshape(rows // dilation, dilation, H, HD)
        return jnp.take_along_axis(shaped, choose[None, None, :, None], axis=1)[:, 0]

    def gathered(data):
        flat = lax.all_gather(select(data).reshape(-1, D), "seq", axis=0, tiled=True)
        return flat.reshape(-1, H, HD)

    keys, values = gathered(key_rows), gathered(value_rows)
    scores = jnp.einsum("qhd,khd->hqk", select(queries), keys, preferred_element_type=F32) * SCALE
    top = jnp.max(scores, axis=-1, keepdims=True)
    expo = jnp.exp(scores - top)
    total = jnp.sum(expo, axis=-1)
    mixed = jnp.einsum("hqk,khd->qhd", expo.astype(BF), values, preferred_element_type=F32)
    mixed = mixed / jnp.transpose(total)[:, :, None]
    lse = jnp.transpose(top[..., 0] + jnp.log(total))
    selected = jnp.arange(dilation)[:, None] == choose[None, :]
    full_mixed = jnp.where(selected[None, :, :, None], mixed[:, None], F32(0.0)).reshape(rows, D)
    full_lse = jnp.where(selected[None], lse[:, None], F32(-1e30)).reshape(rows, H)
    full_lse = jnp.repeat(full_lse, HD, axis=1)

    def tiled(data):
        return data.reshape(rows, D // TILE, TILE).swapaxes(0, 1)

    return tiled(full_mixed), tiled(full_lse)


def exchange(blocks):
    count = lax.axis_size("seq")
    teams = None
    if count != MID_SPAN:
        teams = [[first + i for i in range(MID_SPAN)] for first in range(0, count, MID_SPAN)]
    return lax.all_to_all(blocks, "seq", 0, 0, axis_index_groups=teams, tiled=True)


def shards(queries, key_rows, value_rows, offsets):
    rows = queries.shape[0]
    count = lax.axis_size("seq")
    wide = 2 if count == MID_SPAN else 1
    groups = rows // MID_SPAN
    near_rows = rows // NEAR_SPAN
    send_rows = H * 3 * groups
    back_rows = H * groups
    smem = pl.BlockSpec(memory_space=pltpu.SMEM)
    vmem = pl.BlockSpec(memory_space=pltpu.VMEM)
    hbm = pl.BlockSpec(memory_space=pltpu.HBM)
    shape = jax.ShapeDtypeStruct

    def sems(*count):
        return pltpu.SemaphoreType.DMA(count)

    near_q, near_kv, send = pl.pallas_call(
        functools.partial(prep_kernel, wide),
        out_shape=(
            shape((near_rows, D), BF),
            shape((2 * near_rows, D), BF),
            shape((send_rows, TILE), BF),
        ),
        in_specs=[smem, hbm, hbm, hbm],
        out_specs=(hbm, hbm, hbm),
        scratch_shapes=[
            pltpu.VMEM((3, rows, D), BF),
            pltpu.VMEM((3, D // TILE, rows, TILE), F32),
            pltpu.VMEM((near_rows, D), BF),
            pltpu.VMEM((2 * near_rows, D), BF),
            pltpu.VMEM((send_rows, TILE), BF),
            sems(PARTS * 3),
            sems(PARTS, 3),
        ],
        compiler_params=params(),
        cost_estimate=cost(6 * rows * D, 10 * rows * D),
        name="prep",
    )(offsets, queries, key_rows, value_rows)

    near_side = from_partner(near_kv, "seq", 2)
    near_core = from_partner(near_kv, "seq", 1)
    recv = exchange(send)

    tiled = (2, D // TILE, rows, TILE)
    own = pl.pallas_call(
        local_kernel,
        out_shape=shape(tiled, F32),
        in_specs=[hbm] * 3,
        out_specs=hbm,
        scratch_shapes=[pltpu.VMEM((3, rows, D), BF), pltpu.VMEM(tiled, F32), sems(PARTS * 3), sems(PARTS, 2 * PART_TILES)],
        compiler_params=params(),
        cost_estimate=cost(400 * rows * rows * H * 256, 14 * rows * D, rows * rows * H),
        name="local",
    )(queries, key_rows, value_rows)
    own, recv, near_side = lax.optimization_barrier((own, recv, near_side))

    near_both = from_partner(near_side, "seq", 1)
    back = pl.pallas_call(
        functools.partial(owned_kernel, wide),
        out_shape=shape((back_rows, TILE), BF),
        in_specs=[vmem],
        out_specs=hbm,
        scratch_shapes=[pltpu.VMEM((back_rows, TILE), BF), sems(1)],
        compiler_params=params(OWNED_BYTES),
        cost_estimate=cost(4 * wide * rows * rows * 256, 2 * send_rows * TILE, wide * rows * rows),
        name="owned",
    )(recv)
    back = exchange(back)

    if wide == 1:
        far_branch, far_lse = far_by_gather(queries, key_rows, value_rows, offsets[2], count)
        own = jnp.stack(combine(own[0], own[1], far_branch, far_lse))
    state = pl.pallas_call(
        functools.partial(near_kernel, wide),
        out_shape=shape((12 * D // TILE, rows, TILE), F32),
        in_specs=[smem] + [hbm] * (2 + NEAR_SPAN),
        out_specs=hbm,
        scratch_shapes=[
            pltpu.VMEM((near_rows, D), BF),
            pltpu.VMEM((2, NEAR_SPAN * near_rows, D), BF),
            pltpu.VMEM(tiled, F32),
            pltpu.VMEM((D // TILE, 2 * wide * groups, TILE), F32),
            sems(PARTS, 1 + 2 * NEAR_SPAN),
            sems(PARTS, 2 * PART_TILES),
            sems(PARTS, 2 * PART_TILES),
        ],
        compiler_params=params(),
        cost_estimate=cost(4 * near_rows * rows * H * 256, 8 * rows * D, near_rows * rows * H),
        name="near",
    )(offsets, near_q, near_kv, near_core, near_side, near_both, own)
    state, back = lax.optimization_barrier((state, back))

    return pl.pallas_call(
        functools.partial(merge_kernel, wide),
        out_shape=shape((rows, D), BF),
        in_specs=[smem, vmem, hbm],
        out_specs=hbm,
        scratch_shapes=[
            pltpu.VMEM((D // TILE, rows, TILE), F32),
            pltpu.VMEM((D // TILE, 2 * wide * groups, TILE), F32),
            pltpu.VMEM((rows, D), BF),
            sems(PARTS, 2 * PART_TILES),
            sems(PARTS, 1),
        ],
        compiler_params=params(SMALL_BYTES),
        cost_estimate=cost(2 * rows * rows * D, 14 * rows * D),
        name="merge",
    )(offsets, back, state)


def solution(mesh):
    in_specs = (
        P(("slides", "seq"), None),
        P(("slides", "seq"), None),
        P(("slides", "seq"), None),
        P(),
    )
    out_specs = P(("slides", "seq"), None)
    return jax.shard_map(shards, mesh=mesh, in_specs=in_specs, out_specs=out_specs, check_vma=False)
```

profile of v0, /device:TPU:0, one launch (start us, length us, event | category | flops | bytes accessed | tf_op | source)
XLA Modules:
  0.0 44.1 jit_solution(11953760217426249304)
XLA Ops:
  0.0 4.7 %prep.1 = (bf16[128,768]{1,0:T(8,128)(2,1)}, bf16[256,768]{1,0:T(8,128)(2,1)}, bf16[1536,128]{1,0:T(8,128)(2,1)}) custom-call(s32[3,16]{1,0:T(4,128)} %offsets_ref.5, bf16[512,768]{1,0:T(8,128)(2,1)} %q_ref.3, bf16[512,768]{1,0:T(8,128)(2,1)} %k_ref.3, bf16[512,768]{1,0:T(8,128)(2,1)} %v_ref.3), custom_call_target="tpu_custom_call" | custom-call | flops 2359296 | bytes 3932160 | tf_op jit(solution)/shard_map/prep/pallas_call | solution.py:467
  4.8 3.0 %collective-permute-start.1 = (bf16[256,768]{1,0:T(8,128)(2,1)}, bf16[256,768]{1,0:T(8,128)(2,1)}, u32[]{:S(2)}, u32[]{:S(2)}) collective-permute-start(bf16[256,768]{1,0:T(8,128)(2,1)} %get-tuple-element.14.refs_0_), channel_id=1, source_target_pairs={{0,2},{1,3},{2,0},{3,1},{4,6},{5,7},{6,4},{7,5},{8,10},{9,11},{10,... | collective-permute-start | bytes 1179656 | tf_op jit(solution)/shard_map/ppermute | solution.py:32
  7.8 0.0 collective-permute-start
  7.8 5.1 %all-to-all-start = ((bf16[16,96,128]{2,1,0:T(8,128)(2,1)}), bf16[16,96,128]{2,1,0:T(8,128)(2,1)}, u32[]{:S(2)}, u32[]{:S(2)}) async-start(bf16[16,96,128]{2,1,0:T(8,128)(2,1)} %bitcast.5), calls=%async_computation | async-start | bytes 786432 | tf_op jit(solution)/shard_map/all_to_all | solution.py:448
  12.9 8.7 %local.1.refs_4_ = f32[2,6,512,128]{3,2,1,0:T(8,128)} custom-call(bf16[512,768]{1,0:T(8,128)(2,1)} %q_ref.3, bf16[512,768]{1,0:T(8,128)(2,1)} %k_ref.3, bf16[512,768]{1,0:T(8,128)(2,1)} %v_ref.3), custom_call_target="tpu_custom_call" | custom-call | flops 429496729600 | bytes 5505024 | tf_op jit(solution)/shard_map/local/pallas_call | solution.py:495
  21.7 0.0 copy-start
  21.7 0.0 collective-permute-done.1.refs_2_
  21.7 3.5 %all-to-all-done = bf16[16,96,128]{2,1,0:T(8,128)(2,1)} async-done(((bf16[16,96,128]{2,1,0:T(8,128)(2,1)}), bf16[16,96,128]{2,1,0:T(8,128)(2,1)}, u32[]{:S(2)}, u32[]{:S(2)}) %all-to-all-start) | async-done | bytes 393248 | tf_op jit(solution)/shard_map/all_to_all | solution.py:448
  25.2 0.1 collective-permute-start.2
  25.3 3.0 %owned.1 = bf16[512,128]{1,0:T(8,128)(2,1)} custom-call(bf16[1536,128]{1,0:T(8,128)(2,1)} %bitcast.1.recv_ref), custom_call_target="tpu_custom_call" | custom-call | flops 536870912 | bytes 393216 | tf_op jit(solution)/shard_map/owned/pallas_call | solution.py:508
  28.3 3.7 %all-to-all-start.1 = ((bf16[16,32,128]{2,1,0:T(8,128)(2,1)}), bf16[16,32,128]{2,1,0:T(8,128)(2,1)S(1)}, u32[]{:S(2)}, u32[]{:S(2)}) async-start(bf16[16,32,128]{2,1,0:T(8,128)(2,1)} %bitcast.2), calls=%async_computation.1 | async-start | bytes 262144 | tf_op jit(solution)/shard_map/all_to_all | solution.py:448
  32.1 0.0 collective-permute-done.refs_1_
  32.1 0.0 collective-permute-done.2.refs_3_
  32.1 0.0 copy-start.1
  32.1 0.8 %copy-done.1 = bf16[256,768]{1,0:T(8,128)(2,1)} copy-done((bf16[256,768]{1,0:T(8,128)(2,1)}, bf16[256,768]{1,0:T(8,128)(2,1)S(1)}, u32[]{:S(2)}) %copy-start.1) | copy-done | bytes 393240
  32.9 7.2 %near.1.state_ref = f32[72,512,128]{2,1,0:T(8,128)} custom-call(s32[3,16]{1,0:T(4,128)} %offsets_ref.5, bf16[128,768]{1,0:T(8,128)(2,1)} %get-tuple-element.13.q_ref, bf16[256,768]{1,0:T(8,128)(2,1)} %get-tuple-element.14.refs_0_, bf16[256,768]{1,0:T(8,128)(2,1)} %collective-permute-done.refs_1_, bf16[256,768]{1,0:T(8,128)(2,1)} %collective-permute-done.1.refs_2_, ...), custom_call_target="tpu_custom_call" | custom-call | flops 1073741824 | bytes 3145728 | tf_op jit(solution)/shard_map/near/pallas_call | solution.py:523
  40.1 0.0 all-to-all-done.1
  40.1 0.0 copy-done
  40.1 3.9 %merge.1 = bf16[512,768]{1,0:T(8,128)(2,1)} custom-call(s32[3,16]{1,0:T(4,128)S(1)} %copy-done, bf16[512,128]{1,0:T(8,128)(2,1)S(1)} %bitcast.4, f32[72,512,128]{2,1,0:T(8,128)} %near.1.state_ref), custom_call_target="tpu_custom_call" | custom-call | flops 402653184 | bytes 5505024 | tf_op jit(solution)/shard_map/merge/pallas_call | solution.py:543
Async XLA Ops:
  4.8 16.9 %collective-permute-start.1 = (bf16[256,768]{1,0:T(8,128)(2,1)}, bf16[256,768]{1,0:T(8,128)(2,1)}, u32[]{:S(2)}, u32[]{:S(2)}) collective-permute-start(bf16[256,768]{1,0:T(8,128)(2,1)} %get-tuple-element.14.refs_0_), channel_id=1, source_target_pairs={{0,2},{1,3},{2,0},{3,1},{4,6},{5,7},{6,4},{7,5},{8,10},{9,11},{10,... | collective-permute-start | bytes 1179656 | tf_op jit(solution)/shard_map/ppermute | solution.py:32
  7.8 24.3 %collective-permute-start = (bf16[256,768]{1,0:T(8,128)(2,1)}, bf16[256,768]{1,0:T(8,128)(2,1)}, u32[]{:S(2)}, u32[]{:S(2)}) collective-permute-start(bf16[256,768]{1,0:T(8,128)(2,1)} %get-tuple-element.14.refs_0_), channel_id=1, source_target_pairs={{0,1},{1,0},{2,3},{3,2},{4,5},{5,4},{6,7},{7,6},{8,9},{9,8},{10,11... | collective-permute-start | bytes 1179656 | tf_op jit(solution)/shard_map/ppermute | solution.py:32
  7.8 17.4 %all-to-all-start = ((bf16[16,96,128]{2,1,0:T(8,128)(2,1)}), bf16[16,96,128]{2,1,0:T(8,128)(2,1)}, u32[]{:S(2)}, u32[]{:S(2)}) async-start(bf16[16,96,128]{2,1,0:T(8,128)(2,1)} %bitcast.5), calls=%async_computation | async-start | bytes 786432 | tf_op jit(solution)/shard_map/all_to_all | solution.py:448
  21.7 18.4 %copy-start = (s32[3,16]{1,0:T(4,128)S(1)}, s32[3,16]{1,0:T(4,128)}, u32[]{:S(2)}) copy-start(s32[3,16]{1,0:T(4,128)} %offsets_ref.5) | copy-start | bytes 580
  25.2 6.9 %collective-permute-start.2 = (bf16[256,768]{1,0:T(8,128)(2,1)}, bf16[256,768]{1,0:T(8,128)(2,1)S(1)}, u32[]{:S(2)}, u32[]{:S(2)}) collective-permute-start(bf16[256,768]{1,0:T(8,128)(2,1)} %collective-permute-done.1.refs_2_), channel_id=1, source_target_pairs={{0,1},{1,0},{2,3},{3,2},{4,5},{5,4},{6,7},{7,6},{8,9},{9,8},{10,11... | collective-permute-start | bytes 1179656 | tf_op jit(solution)/shard_map/ppermute | solution.py:32
  28.3 11.8 %all-to-all-start.1 = ((bf16[16,32,128]{2,1,0:T(8,128)(2,1)}), bf16[16,32,128]{2,1,0:T(8,128)(2,1)S(1)}, u32[]{:S(2)}, u32[]{:S(2)}) async-start(bf16[16,32,128]{2,1,0:T(8,128)(2,1)} %bitcast.2), calls=%async_computation.1 | async-start | bytes 262144 | tf_op jit(solution)/shard_map/all_to_all | solution.py:448
  32.1 0.8 %copy-start.1 = (bf16[256,768]{1,0:T(8,128)(2,1)}, bf16[256,768]{1,0:T(8,128)(2,1)S(1)}, u32[]{:S(2)}) copy-start(bf16[256,768]{1,0:T(8,128)(2,1)S(1)} %collective-permute-done.2.refs_3_) | copy-start | bytes 1179652
where the time goes:
time: 44.6 us; the launch traced here: 44.1 us
  Pallas kernels  27.6 us (62%)
  starting transfers between devices  12 us (27%)
  waiting for transfers between devices  3.5 us (8%)
  local copies, waits for them, and re-layouts  0.76 us (2%)
    all_to_all x2, starting transfers between devices, exchange(): lax.all_to_all(blocks, 'seq', 0, 0, axis_index_groups=teams, tiled=True)  8.88 us
    pallas_call x1, Pallas kernels, shards(): pl.pallas_call(local_kernel, out_shape=shape(tiled, F32), in_specs=[hbm]...  8.74 us
    pallas_call x1, Pallas kernels, shards(): pl.pallas_call(functools.partial(near_kernel, wide), out_shape=shape((12...  7.23 us
    pallas_call x1, Pallas kernels, shards(): pl.pallas_call(functools.partial(prep_kernel, wide), out_shape=(shape((ne...  4.74 us
    pallas_call x1, Pallas kernels, shards(): pl.pallas_call(functools.partial(merge_kernel, wide), out_shape=shape((ro...  3.85 us
    all_to_all x2, waiting for transfers between devices, exchange(): lax.all_to_all(blocks, 'seq', 0, 0, axis_index_groups=teams, tiled=True)  3.49 us
    ppermute x3, starting transfers between devices, from_partner(): return lax.ppermute(block, axis, [(i, i ^ flip) for i in range(count)])  3.15 us
    pallas_call x1, Pallas kernels, shards(): pl.pallas_call(functools.partial(owned_kernel, wide), out_shape=shape((ba...  3.02 us
  transfers between devices with their start and end apart: 5, of which 1 were waited for; matrix products, arithmetic and copies ran while one was open for 0% of the time, Pallas kernels for 43%

commit v1 on v0

--- a/solution.py
+++ b/solution.py
@@ -18,6 +18,9 @@
 PARTS = D // HALF
 PART_TILES = HALF // TILE
 STAT_LANE = (2 * HD, 2 * HD + 16)
+SPARE = TILE - 2 * HD
+SECTION = 256
+PITCH = 36
 SCALE = HD ** (-0.5)
 LOG2E = 1.4426950408889634
 VMEM_BYTES = 63 * 1024 * 1024
@@ -61,8 +64,8 @@
     return range(head * HD // TILE, ((head + 1) * HD - 1) // TILE + 1)
 
 
-def every(first, rows):
-    return pl.ds(first, rows // MID_SPAN, stride=MID_SPAN)
+def every(first, chunk):
+    return pl.ds(first + MID_SPAN * 8 * chunk, 8, stride=MID_SPAN)
 
 
 def bits_of(offs, count):
@@ -73,6 +76,10 @@
     for bit in bits:
         blocks = [jnp.where(bit, high, low) for low, high in zip(blocks[::2], blocks[1::2])]
     return blocks[0]
+
+
+def tile_lanes(tile):
+    return slice(tile * TILE, (tile + 1) * TILE)
 
 
 def lanes_of(part):
@@ -88,6 +95,32 @@
 
 def scale_lane(scale):
     return scale * HD
+
+
+def spare_turn(piece):
+    return (2 * HD - piece * SPARE) % TILE
+
+
+def folded(place, chunks):
+    result = []
+    for first in range(0, len(chunks), 4):
+        last = chunks[first + 3]
+        for piece in range(3):
+            moved = pltpu.roll(last, spare_turn(piece), 1) if spare_turn(piece) else last
+            result.append(jnp.where(place < 2 * HD, chunks[first + piece], moved))
+    return result
+
+
+def unfolded(place, chunks):
+    result = []
+    for first in range(0, len(chunks), 3):
+        last = None
+        for piece in range(3):
+            turn = (TILE - spare_turn(piece)) % TILE
+            moved = pltpu.roll(chunks[first + piece], turn, 1) if turn else chunks[first + piece]
+            last = moved if last is None else jnp.where(place >= piece * SPARE, moved, last)
+        result += chunks[first : first + 3] + [last]
+    return result
 
 
 def prep_kernel(
@@ -97,58 +130,62 @@
     rows = q_ref.shape[0]
     groups = rows // MID_SPAN
     near_rows = rows // NEAR_SPAN
-    arrivals = flights(
-        [
-            (ref.at[:, lanes_of(part)], stage.at[x, :, lanes_of(part)])
-            for part in range(PARTS)
-            for x, ref in enumerate((q_ref, k_ref, v_ref))
-        ],
-        in_sems,
-    )
-    lane = lax.broadcasted_iota(jnp.int32, (groups, TILE), 1)
-    leaving = []
-    for part in range(PARTS):
-        here = lanes_of(part)
-        tiles = range(part * PART_TILES, (part + 1) * PART_TILES)
-        bits = [
-            {t: bits_of(tile_offsets(offsets_ref, s, t, groups), MID_SPAN if s else NEAR_SPAN) for t in tiles}
-            for s in range(1 + wide)
-        ]
+    tiles = range(D // TILE)
+    sections = [slice(c * SECTION, (c + 1) * SECTION) for c in range(rows // SECTION)]
+    arrivals = [
+        flights([(ref.at[section], stage.at[x, section]) for x, ref in enumerate((q_ref, k_ref, v_ref))], in_sems.at[c])
+        for c, section in enumerate(sections)
+    ]
+    lane = lax.broadcasted_iota(jnp.int32, (8, TILE), 1)
+    near_bits = [bits_of(tile_offsets(offsets_ref, 0, t, 8), NEAR_SPAN) for t in tiles]
+    wide_bits = [[bits_of(tile_offsets(offsets_ref, 1 + s, t, 8), MID_SPAN) for t in tiles] for s in range(wide)]
+    chosen = {}
+    for c, section in enumerate(sections):
+        kept = SECTION // MID_SPAN
         for x in range(3):
-            arrivals[part * 3 + x].wait()
-            chosen = [{} for _ in range(wide)]
+            arrivals[c][x].wait()
             for t in tiles:
-                lanes = slice(t * TILE, (t + 1) * TILE)
-                single[x, t] = stage[x, :, lanes].astype(F32)
-                block = [single[x, t, every(o, rows), :] for o in range(MID_SPAN)]
+                lanes = tile_lanes(t)
+                spread = stage[x, section, lanes].astype(F32)
+                for g in range(kept):
+                    for i in range(2):
+                        at = g * MID_SPAN + 8 * i
+                        single[x, t, pl.ds(c * kept + g + 8 * i * PITCH, 8, stride=PITCH), :] = spread[at : at + 8]
+                near_parts = [[] for _ in range(NEAR_SPAN)]
+                for chunk in range(c * kept // 8, (c + 1) * kept // 8):
+                    block = [single[x, t, o * PITCH + 8 * chunk : o * PITCH + 8 * chunk + 8, :] for o in range(MID_SPAN)]
+                    for a in range(NEAR_SPAN):
+                        near_parts[a].append(pick(block[a * NEAR_SPAN : (a + 1) * NEAR_SPAN], near_bits[t]))
+                    for s in range(wide):
+                        picked = pick(block, wide_bits[s][t])
+                        chosen[x, s, t, chunk] = pltpu.roll(picked, scale_lane(s), 1) if s else picked
                 for a in range(NEAR_SPAN):
-                    picked = pick(block[a * NEAR_SPAN : (a + 1) * NEAR_SPAN], bits[0][t]).astype(BF)
+                    near_block = jnp.concatenate(near_parts[a], axis=0).astype(BF)
+                    base = a * groups + c * kept
                     if x == 0:
-                        near_q[a * groups : (a + 1) * groups, lanes] = picked
+                        near_q[base : base + kept, lanes] = near_block
                     else:
-                        base = (x - 1) * near_rows + a * groups
-                        near[base : base + groups, lanes] = picked
-                for s in range(wide):
-                    picked = pick(block, bits[1 + s][t])
-                    chosen[s][t] = pltpu.roll(picked, scale_lane(s), 1) if s else picked
-            for h in range(part * HALF_HEADS, (part + 1) * HALF_HEADS):
-                travel = jnp.zeros((groups, TILE), F32)
+                        base += (x - 1) * near_rows
+                        near[base : base + kept, lanes] = near_block
+    leaving = flights([(near, near_out), (near_q, near_q_out)], out_sems.at[0])
+    for h in range(H):
+        travel = []
+        for x in range(3):
+            chunks = []
+            for chunk in range(groups // 8):
+                joined = jnp.zeros((8, TILE), F32)
                 for s in range(wide):
                     for t in tiles_of(h):
                         low, high = max(h * HD, t * TILE), min((h + 1) * HD, (t + 1) * TILE)
                         turned = (lane - scale_lane(s)) & (TILE - 1)
                         hit = (turned >= low - t * TILE) & (turned < high - t * TILE)
-                        travel = jnp.where(hit, chosen[s][t], travel)
-                send[h * 3 * groups + x * groups : h * 3 * groups + (x + 1) * groups, :] = travel.astype(BF)
-        owners = slice(part * HALF_HEADS * 3 * groups, (part + 1) * HALF_HEADS * 3 * groups)
-        leaving += flights(
-            [
-                (send.at[owners], send_out.at[owners]),
-                (near.at[:, here], near_out.at[:, here]),
-                (near_q.at[:, here], near_q_out.at[:, here]),
-            ],
-            out_sems.at[part],
-        )
+                        joined = jnp.where(hit, chosen[x, s, t, chunk], joined)
+                chunks.append(joined)
+            travel += folded((lane - h * HD) & (TILE - 1), chunks)
+        send[h] = jnp.concatenate(travel, axis=0).astype(BF)
+        if h == H // 2 - 1:
+            leaving += flights([(send.at[: H // 2], send_out.at[: H // 2])], out_sems.at[1])
+    leaving += flights([(send.at[H // 2 :], send_out.at[H // 2 :])], out_sems.at[2])
     for copy in leaving:
         copy.wait()
 
@@ -279,27 +316,27 @@
             copy.wait()
         for i in range(PART_TILES):
             t = part * PART_TILES + i
-            branch = [own[0, t, every(o, rows), :] for o in range(MID_SPAN)]
-            lse = [own[1, t, every(o, rows), :] for o in range(MID_SPAN)]
-            offs = tile_offsets(offsets_ref, 0, t, groups)
+            offs = tile_offsets(offsets_ref, 0, t, 8)
             hits, bits = [offs == b for b in range(NEAR_SPAN)], bits_of(offs, NEAR_SPAN)
-            for a in range(NEAR_SPAN):
-                members = slice(a * NEAR_SPAN, (a + 1) * NEAR_SPAN)
-                span = slice(a * groups, (a + 1) * groups)
-                mixed, high = combine(
-                    pick(branch[members], bits), pick(lse[members], bits), near_branch[i][span], near_lse[i][span]
-                )
-                for b, hit in enumerate(hits):
-                    o = a * NEAR_SPAN + b
-                    branch[o] = jnp.where(hit, mixed, branch[o])
-                    lse[o] = jnp.where(hit, high, lse[o])
-            for o in range(MID_SPAN):
-                own[0, t, every(o, rows), :] = branch[o]
-            for s in range(wide):
-                bits = bits_of(tile_offsets(offsets_ref, 1 + s, t, groups), MID_SPAN)
-                for kind, blocks in enumerate((branch, lse)):
-                    base = (2 * s + kind) * groups
-                    picked[t, base : base + groups] = pick(blocks, bits)
+            wide_bits = [bits_of(tile_offsets(offsets_ref, 1 + s, t, 8), MID_SPAN) for s in range(wide)]
+            for chunk in range(groups // 8):
+                branch = [own[0, t, every(o, chunk), :] for o in range(MID_SPAN)]
+                lse = [own[1, t, every(o, chunk), :] for o in range(MID_SPAN)]
+                for a in range(NEAR_SPAN):
+                    members = slice(a * NEAR_SPAN, (a + 1) * NEAR_SPAN)
+                    span = slice(a * groups + chunk * 8, a * groups + (chunk + 1) * 8)
+                    mixed, high = combine(
+                        pick(branch[members], bits), pick(lse[members], bits), near_branch[i][span], near_lse[i][span]
+                    )
+                    for b, hit in enumerate(hits):
+                        o = a * NEAR_SPAN + b
+                        branch[o] = jnp.where(hit, mixed, branch[o])
+                        lse[o] = jnp.where(hit, high, lse[o])
+                        own[0, t, every(o, chunk), :] = branch[o]
+                for s in range(wide):
+                    for kind, blocks in enumerate((branch, lse)):
+                        base = (2 * s + kind) * groups + chunk * 8
+                        picked[t, base : base + 8] = pick(blocks, wide_bits[s])
         tiles = range(part * PART_TILES, (part + 1) * PART_TILES)
         pairs = [(own.at[0, t], state_out.at[t]) for t in tiles]
         pairs += [(picked.at[t], state_out.at[D // TILE + t, : 2 * wide * groups]) for t in tiles]
@@ -309,14 +346,20 @@
 
 
 def owned_kernel(wide, recv_ref, back_out, back, out_sems):
-    groups = recv_ref.shape[0] // (3 * MID_SPAN)
+    third = recv_ref.shape[1] // 3
+    groups = third * 4 // 3
     head = lax.rem(lax.axis_index("seq"), H)
     lane = lax.broadcasted_iota(jnp.int32, (1, TILE), 1)
     row_place = (lane - head * HD) & (TILE - 1)
+    chunk_place = (lax.broadcasted_iota(jnp.int32, (8, TILE), 1) - head * HD) & (TILE - 1)
+    peers = [recv_ref[peer].astype(F32) for peer in range(MID_SPAN)]
 
     def rows_of(x):
-        starts = [(3 * peer + x) * groups for peer in range(MID_SPAN)]
-        return jnp.concatenate([recv_ref[start : start + groups, :] for start in starts], axis=0)
+        found = []
+        for peer in peers:
+            chunks = [peer[r : r + 8] for r in range(x * third, (x + 1) * third, 8)]
+            found += unfolded(chunk_place, chunks)
+        return jnp.concatenate(found, axis=0).astype(BF)
 
     q, k, v = (rows_of(x) for x in range(3))
     full_lane = lax.broadcasted_iota(jnp.int32, (q.shape[0], TILE), 1)
@@ -354,14 +397,15 @@
 def merge_kernel(wide, offsets_ref, back_ref, state_ref, out_ref, base, picked, out, in_sems, out_sems):
     rows = out_ref.shape[0]
     groups = rows // MID_SPAN
-    arrivals = []
-    for part in range(PARTS):
-        tiles = range(part * PART_TILES, (part + 1) * PART_TILES)
-        pairs = [(state_ref.at[D // TILE + t, : 2 * wide * groups], picked.at[t]) for t in tiles]
-        pairs += [(state_ref.at[t], base.at[t]) for t in tiles]
-        arrivals.append(flights(pairs, in_sems.at[part]))
+    arrivals = [
+        flights(
+            [(state_ref.at[D // TILE + t, : 2 * wide * groups], picked.at[t]), (state_ref.at[t], base.at[t])], in_sems.at[t]
+        )
+        for t in range(D // TILE)
+    ]
     lane = lax.broadcasted_iota(jnp.int32, (1, TILE), 1)
     full_lane = lax.broadcasted_iota(jnp.int32, (groups, TILE), 1)
+    row_in_16 = lax.broadcasted_iota(jnp.int32, (MID_SPAN, TILE), 0)
     ones = jnp.ones((TILE, TILE), BF)
     branches, lses = [], []
     for s in range(wide):
@@ -383,29 +427,29 @@
         return result
 
     leaving = []
-    for part in range(PARTS):
-        here = lanes_of(part)
-        for copy in arrivals[part]:
-            copy.wait()
-        for t in range(part * PART_TILES, (part + 1) * PART_TILES):
-            offs, results = [], []
-            for s in range(wide):
-                start = 2 * s * groups
-                branch, lse = picked[t, start : start + groups], picked[t, start + groups : start + 2 * groups]
-                offs.append(tile_offsets(offsets_ref, 1 + s, t, groups))
-                for before, (other_branch, other_lse) in zip(offs, results):
-                    branch = jnp.where(before == offs[s], other_branch, branch)
-                    lse = jnp.where(before == offs[s], other_lse, lse)
-                wide_branch = by_tile(t, lambda h: branches[s][h])
-                wide_lse = by_tile(t, lambda h: lses[s][h * groups : (h + 1) * groups])
-                results.append(combine(branch, lse, wide_branch, wide_lse))
-            for o in range(MID_SPAN):
-                block = base[t, every(o, rows), :]
-                for off, (branch, _) in zip(offs, results):
-                    block = jnp.where(off == o, branch, block)
-                base[t, every(o, rows), :] = block
-            out[:, t * TILE : (t + 1) * TILE] = base[t].astype(BF)
-        leaving += flights([(out.at[:, here], out_ref.at[:, here])], out_sems.at[part])
+    for t in range(D // TILE):
+        lanes = tile_lanes(t)
+        arrivals[t][0].wait()
+        offs, results = [], []
+        for s in range(wide):
+            start = 2 * s * groups
+            branch, lse = picked[t, start : start + groups], picked[t, start + groups : start + 2 * groups]
+            offs.append(tile_offsets(offsets_ref, 1 + s, t, MID_SPAN))
+            for before, (other_branch, other_lse) in zip(offs, results):
+                same = jnp.concatenate([before - offs[s]] * (groups // MID_SPAN), axis=0) == 0
+                branch = jnp.where(same, other_branch, branch)
+                lse = jnp.where(same, other_lse, lse)
+            wide_branch = by_tile(t, lambda h: branches[s][h])
+            wide_lse = by_tile(t, lambda h: lses[s][h * groups : (h + 1) * groups])
+            results.append(combine(branch, lse, wide_branch, wide_lse))
+        hits = [row_in_16 == off for off in offs]
+        arrivals[t][1].wait()
+        for g in range(groups):
+            block = base[t, g * MID_SPAN : (g + 1) * MID_SPAN]
+            for hit, (branch, _) in zip(hits, results):
+                block = jnp.where(hit, jnp.broadcast_to(branch[g : g + 1], (MID_SPAN, TILE)), block)
+            out[g * MID_SPAN : (g + 1) * MID_SPAN, lanes] = block.astype(BF)
+        leaving += flights([(out.at[:, lanes], out_ref.at[:, lanes])], out_sems.at[t])
     for copy in leaving:
         copy.wait()
 
@@ -454,7 +498,7 @@
     wide = 2 if count == MID_SPAN else 1
     groups = rows // MID_SPAN
     near_rows = rows // NEAR_SPAN
-    send_rows = H * 3 * groups
+    send_shape = (H, 3 * groups * 3 // 4, TILE)
     back_rows = H * groups
     smem = pl.BlockSpec(memory_space=pltpu.SMEM)
     vmem = pl.BlockSpec(memory_space=pltpu.VMEM)
@@ -469,18 +513,18 @@
         out_shape=(
             shape((near_rows, D), BF),
             shape((2 * near_rows, D), BF),
-            shape((send_rows, TILE), BF),
+            shape(send_shape, BF),
         ),
         in_specs=[smem, hbm, hbm, hbm],
         out_specs=(hbm, hbm, hbm),
         scratch_shapes=[
             pltpu.VMEM((3, rows, D), BF),
-            pltpu.VMEM((3, D // TILE, rows, TILE), F32),
+            pltpu.VMEM((3, D // TILE, MID_SPAN * PITCH, TILE), F32),
             pltpu.VMEM((near_rows, D), BF),
             pltpu.VMEM((2 * near_rows, D), BF),
-            pltpu.VMEM((send_rows, TILE), BF),
-            sems(PARTS * 3),
-            sems(PARTS, 3),
+            pltpu.VMEM(send_shape, BF),
+            sems(rows // SECTION, 3),
+            sems(3, 2),
         ],
         compiler_params=params(),
         cost_estimate=cost(6 * rows * D, 10 * rows * D),
@@ -499,7 +543,7 @@
         out_specs=hbm,
         scratch_shapes=[pltpu.VMEM((3, rows, D), BF), pltpu.VMEM(tiled, F32), sems(PARTS * 3), sems(PARTS, 2 * PART_TILES)],
         compiler_params=params(),
-        cost_estimate=cost(400 * rows * rows * H * 256, 14 * rows * D, rows * rows * H),
+        cost_estimate=cost(16 * rows * rows * H * 256, 14 * rows * D, rows * rows * H),
         name="local",
     )(queries, key_rows, value_rows)
     own, recv, near_side = lax.optimization_barrier((own, recv, near_side))
@@ -512,7 +556,7 @@
         out_specs=hbm,
         scratch_shapes=[pltpu.VMEM((back_rows, TILE), BF), sems(1)],
         compiler_params=params(OWNED_BYTES),
-        cost_estimate=cost(4 * wide * rows * rows * 256, 2 * send_rows * TILE, wide * rows * rows),
+        cost_estimate=cost(4 * wide * rows * rows * 256, 4 * rows * D, wide * rows * rows),
         name="owned",
     )(recv)
     back = exchange(back)
@@ -549,8 +593,8 @@
             pltpu.VMEM((D // TILE, rows, TILE), F32),
             pltpu.VMEM((D // TILE, 2 * wide * groups, TILE), F32),
             pltpu.VMEM((rows, D), BF),
-            sems(PARTS, 2 * PART_TILES),
-            sems(PARTS, 1),
+            sems(D // TILE, 2),
+            sems(D // TILE, 1),
         ],
         compiler_params=params(SMALL_BYTES),
         cost_estimate=cost(2 * rows * rows * D, 14 * rows * D),

time: 44.6 us -> 40.7 us (0.913)
  Pallas kernels: 27.6 us -> 24.8 us
  waiting for transfers between devices: 3.5 us -> 1.79 us
  starting transfers between devices: 12 us -> 12.6 us
    all_to_all x2, waiting for transfers between devices: 3.49 us -> 1.78 us  [exchange(): lax.all_to_all(blocks, 'seq', 0, 0, axis_index_groups=teams, tiled=True)]
    pallas_call x1, Pallas kernels: 4.74 us -> 3.82 us  [shards(): pl.pallas_call(functools.partial(prep_kernel, wide), out_shape=(shape((ne...]
    pallas_call x1, Pallas kernels: 3.85 us -> 2.93 us  [shards(): pl.pallas_call(functools.partial(merge_kernel, wide), out_shape=shape((ro...]
    pallas_call x1, Pallas kernels: 3.02 us -> 2.15 us  [shards(): pl.pallas_call(functools.partial(owned_kernel, wide), out_shape=shape((ba...]
    all_to_all x2, starting transfers between devices: 8.88 us -> 9.57 us  [exchange(): lax.all_to_all(blocks, 'seq', 0, 0, axis_index_groups=teams, tiled=True)]
  transfers between devices with their start and end apart: 5 -> 5, of which waited for: 1 -> 1; matrix products, arithmetic and copies ran while one was open for 0% -> 0% of each run, Pallas kernels for 43% -> 45%
where the time goes in v1:
time: 40.7 us; the launch traced here: 40.3 us
  Pallas kernels  24.8 us (61%)
  starting transfers between devices  12.6 us (31%)
  waiting for transfers between devices  1.79 us (4%)
  local copies, waits for them, and re-layouts  0.78 us (2%)
    all_to_all x2, starting transfers between devices, exchange(): lax.all_to_all(blocks, 'seq', 0, 0, axis_index_groups=teams, tiled=True)  9.57 us
    pallas_call x1, Pallas kernels, shards(): pl.pallas_call(local_kernel, out_shape=shape(tiled, F32), in_specs=[hbm]...  8.75 us
    pallas_call x1, Pallas kernels, shards(): pl.pallas_call(functools.partial(near_kernel, wide), out_shape=shape((12...  7.19 us
    pallas_call x1, Pallas kernels, shards(): pl.pallas_call(functools.partial(prep_kernel, wide), out_shape=(shape((ne...  3.82 us
    ppermute x3, starting transfers between devices, from_partner(): return lax.ppermute(block, axis, [(i, i ^ flip) for i in range(count)])  3.04 us
    pallas_call x1, Pallas kernels, shards(): pl.pallas_call(functools.partial(merge_kernel, wide), out_shape=shape((ro...  2.93 us
    pallas_call x1, Pallas kernels, shards(): pl.pallas_call(functools.partial(owned_kernel, wide), out_shape=shape((ba...  2.15 us
    all_to_all x2, waiting for transfers between devices, exchange(): lax.all_to_all(blocks, 'seq', 0, 0, axis_index_groups=teams, tiled=True)  1.78 us
  transfers between devices with their start and end apart: 5, of which 1 were waited for; matrix products, arithmetic and copies ran while one was open for 0% of the time, Pallas kernels for 45%

profile of v1, /device:TPU:0, one launch (start us, length us, event | category | flops | bytes accessed | tf_op | source)
XLA Modules:
  0.0 40.3 jit_solution(8298324642779438283)
XLA Ops:
  0.0 3.8 %prep.1 = (bf16[128,768]{1,0:T(8,128)(2,1)}, bf16[256,768]{1,0:T(8,128)(2,1)}, bf16[16,72,128]{2,1,0:T(8,128)(2,1)}) custom-call(s32[3,16]{1,0:T(4,128)} %offsets_ref.5, bf16[512,768]{1,0:T(8,128)(2,1)} %q_ref.3, bf16[512,768]{1,0:T(8,128)(2,1)} %k_ref.3, bf16[512,768]{1,0:T(8,128)(2,1)} %v_ref.3), custom_call_target="tpu_custom_call" | custom-call | flops 2359296 | bytes 3932160 | tf_op jit(solution)/shard_map/prep/pallas_call | solution.py:511
  3.8 3.0 %collective-permute-start.1 = (bf16[256,768]{1,0:T(8,128)(2,1)}, bf16[256,768]{1,0:T(8,128)(2,1)S(1)}, u32[]{:S(2)}, u32[]{:S(2)}) collective-permute-start(bf16[256,768]{1,0:T(8,128)(2,1)} %get-tuple-element.14.refs_0_), channel_id=1, source_target_pairs={{0,2},{1,3},{2,0},{3,1},{4,6},{5,7},{6,4},{7,5},{8,10},{9,11},{10,... | collective-permute-start | bytes 1179656 | tf_op jit(solution)/shard_map/ppermute | solution.py:35
  6.9 0.0 collective-permute-start
  6.9 5.1 %all-to-all-start = ((bf16[16,72,128]{2,1,0:T(8,128)(2,1)}), bf16[16,72,128]{2,1,0:T(8,128)(2,1)S(1)}, u32[]{:S(2)}, u32[]{:S(2)}) async-start(bf16[16,72,128]{2,1,0:T(8,128)(2,1)} %get-tuple-element.15), calls=%async_computation | async-start | bytes 589824 | tf_op jit(solution)/shard_map/all_to_all | solution.py:492
  12.0 8.8 %local.1.refs_4_ = f32[2,6,512,128]{3,2,1,0:T(8,128)} custom-call(bf16[512,768]{1,0:T(8,128)(2,1)} %q_ref.3, bf16[512,768]{1,0:T(8,128)(2,1)} %k_ref.3, bf16[512,768]{1,0:T(8,128)(2,1)} %v_ref.3), custom_call_target="tpu_custom_call" | custom-call | flops 17179869184 | bytes 5505024 | tf_op jit(solution)/shard_map/local/pallas_call | solution.py:539
  20.7 0.0 copy-start
  20.7 0.0 collective-permute-done.1.refs_2_
  20.8 0.0 copy-start.1
  20.8 1.8 %all-to-all-done.recv_ref = bf16[16,72,128]{2,1,0:T(8,128)(2,1)S(1)} async-done(((bf16[16,72,128]{2,1,0:T(8,128)(2,1)}), bf16[16,72,128]{2,1,0:T(8,128)(2,1)S(1)}, u32[]{:S(2)}, u32[]{:S(2)}) %all-to-all-start) | async-done | bytes 294944 | tf_op jit(solution)/shard_map/all_to_all | solution.py:492
  22.5 0.0 collective-permute-start.2
  22.5 2.2 %owned.1 = bf16[512,128]{1,0:T(8,128)(2,1)} custom-call(bf16[16,72,128]{2,1,0:T(8,128)(2,1)S(1)} %all-to-all-done.recv_ref), custom_call_target="tpu_custom_call" | custom-call | flops 536870912 | bytes 1572864 | tf_op jit(solution)/shard_map/owned/pallas_call | solution.py:552
  24.7 4.5 %all-to-all-start.1 = ((bf16[16,32,128]{2,1,0:T(8,128)(2,1)}), bf16[16,32,128]{2,1,0:T(8,128)(2,1)S(1)}, u32[]{:S(2)}, u32[]{:S(2)}) async-start(bf16[16,32,128]{2,1,0:T(8,128)(2,1)} %bitcast), calls=%async_computation.1 | async-start | bytes 262144 | tf_op jit(solution)/shard_map/all_to_all | solution.py:492
  29.2 0.0 collective-permute-done.refs_1_
  29.2 0.0 collective-permute-done.2.refs_3_
  29.2 0.0 copy-start.2
  29.2 0.8 %copy-done.2 = bf16[256,768]{1,0:T(8,128)(2,1)} copy-done((bf16[256,768]{1,0:T(8,128)(2,1)}, bf16[256,768]{1,0:T(8,128)(2,1)S(1)}, u32[]{:S(2)}) %copy-start.2) | copy-done | bytes 393240
  30.0 0.0 copy-done.1
  30.0 7.2 %near.1.state_ref = f32[72,512,128]{2,1,0:T(8,128)} custom-call(s32[3,16]{1,0:T(4,128)} %offsets_ref.5, bf16[128,768]{1,0:T(8,128)(2,1)} %get-tuple-element.13.q_ref, bf16[256,768]{1,0:T(8,128)(2,1)} %get-tuple-element.14.refs_0_, bf16[256,768]{1,0:T(8,128)(2,1)} %collective-permute-done.refs_1_, bf16[256,768]{1,0:T(8,128)(2,1)} %copy-done.1, ...), custom_call_target="tpu_custom_call" | custom-call | flops 1073741824 | bytes 3145728 | tf_op jit(solution)/shard_map/near/pallas_call | solution.py:567
  37.2 0.0 all-to-all-done.1
  37.2 0.0 copy-done
  37.2 2.9 %merge.1 = bf16[512,768]{1,0:T(8,128)(2,1)} custom-call(s32[3,16]{1,0:T(4,128)S(1)} %copy-done, bf16[512,128]{1,0:T(8,128)(2,1)S(1)} %bitcast.2, f32[72,512,128]{2,1,0:T(8,128)} %near.1.state_ref), custom_call_target="tpu_custom_call" | custom-call | flops 402653184 | bytes 5505024 | tf_op jit(solution)/shard_map/merge/pallas_call | solution.py:587
Async XLA Ops:
  3.8 16.9 %collective-permute-start.1 = (bf16[256,768]{1,0:T(8,128)(2,1)}, bf16[256,768]{1,0:T(8,128)(2,1)S(1)}, u32[]{:S(2)}, u32[]{:S(2)}) collective-permute-start(bf16[256,768]{1,0:T(8,128)(2,1)} %get-tuple-element.14.refs_0_), channel_id=1, source_target_pairs={{0,2},{1,3},{2,0},{3,1},{4,6},{5,7},{6,4},{7,5},{8,10},{9,11},{10,... | collective-permute-start | bytes 1179656 | tf_op jit(solution)/shard_map/ppermute | solution.py:35
  6.9 22.3 %collective-permute-start = (bf16[256,768]{1,0:T(8,128)(2,1)}, bf16[256,768]{1,0:T(8,128)(2,1)}, u32[]{:S(2)}, u32[]{:S(2)}) collective-permute-start(bf16[256,768]{1,0:T(8,128)(2,1)} %get-tuple-element.14.refs_0_), channel_id=1, source_target_pairs={{0,1},{1,0},{2,3},{3,2},{4,5},{5,4},{6,7},{7,6},{8,9},{9,8},{10,11... | collective-permute-start | bytes 1179656 | tf_op jit(solution)/shard_map/ppermute | solution.py:35
  6.9 15.7 %all-to-all-start = ((bf16[16,72,128]{2,1,0:T(8,128)(2,1)}), bf16[16,72,128]{2,1,0:T(8,128)(2,1)S(1)}, u32[]{:S(2)}, u32[]{:S(2)}) async-start(bf16[16,72,128]{2,1,0:T(8,128)(2,1)} %get-tuple-element.15), calls=%async_computation | async-start | bytes 589824 | tf_op jit(solution)/shard_map/all_to_all | solution.py:492
  20.7 16.5 %copy-start = (s32[3,16]{1,0:T(4,128)S(1)}, s32[3,16]{1,0:T(4,128)}, u32[]{:S(2)}) copy-start(s32[3,16]{1,0:T(4,128)} %offsets_ref.5) | copy-start | bytes 580
  20.8 9.2 %copy-start.1 = (bf16[256,768]{1,0:T(8,128)(2,1)}, bf16[256,768]{1,0:T(8,128)(2,1)S(1)}, u32[]{:S(2)}) copy-start(bf16[256,768]{1,0:T(8,128)(2,1)S(1)} %collective-permute-done.1.refs_2_) | copy-start | bytes 1179652
  22.5 6.7 %collective-permute-start.2 = (bf16[256,768]{1,0:T(8,128)(2,1)S(1)}, bf16[256,768]{1,0:T(8,128)(2,1)S(1)}, u32[]{:S(2)}, u32[]{:S(2)}) collective-permute-start(bf16[256,768]{1,0:T(8,128)(2,1)S(1)} %collective-permute-done.1.refs_2_), channel_id=1, source_target_pairs={{0,1},{1,0},{2,3},{3,2},{4,5},{5,4},{6,7},{7,6},{8,9},{9,8},{10,11... | collective-permute-start | bytes 1179656 | tf_op jit(solution)/shard_map/ppermute | solution.py:35
  24.7 12.5 %all-to-all-start.1 = ((bf16[16,32,128]{2,1,0:T(8,128)(2,1)}), bf16[16,32,128]{2,1,0:T(8,128)(2,1)S(1)}, u32[]{:S(2)}, u32[]{:S(2)}) async-start(bf16[16,32,128]{2,1,0:T(8,128)(2,1)} %bitcast), calls=%async_computation.1 | async-start | bytes 262144 | tf_op jit(solution)/shard_map/all_to_all | solution.py:492
  29.2 0.8 %copy-start.2 = (bf16[256,768]{1,0:T(8,128)(2,1)}, bf16[256,768]{1,0:T(8,128)(2,1)S(1)}, u32[]{:S(2)}) copy-start(bf16[256,768]{1,0:T(8,128)(2,1)S(1)} %collective-permute-done.2.refs_3_) | copy-start | bytes 1179652

commit v2 on v1

--- a/solution.py
+++ b/solution.py
@@ -370,10 +370,14 @@
         low = scale_lane(s)
         columns = inside(row_place, low, low + HD)
         totals = columns + inside(row_place, STAT_LANE[s], STAT_LANE[s] + 3)
-        scores = lax.dot_general(q * columns, k, (((1,), (1,)), ((), ())), preferred_element_type=F32)
-        probs, top = probabilities(scores)
         weights = jnp.concatenate([v * columns, jnp.broadcast_to(totals, v.shape)], axis=1)
-        result = jnp.dot(probs, weights, preferred_element_type=F32)
+        half = q.shape[0] // 2
+        blocks = []
+        for rows in (slice(0, half), slice(half, 2 * half)):
+            scores = lax.dot_general(q[rows] * columns, k, (((1,), (1,)), ((), ())), preferred_element_type=F32)
+            probs, top = probabilities(scores)
+            blocks.append((jnp.dot(probs, weights, preferred_element_type=F32), top))
+        result, top = (jnp.concatenate(both, axis=0) for both in zip(*blocks))
         num_den = result if num_den is None else num_den + result
         tops = jnp.where((place >= STAT_LANE[s]) & (place < STAT_LANE[s] + 3), top, tops)
     den = num_den[:, TILE:]

time: 40.7 us -> 40.4 us (level)
  transfers between devices with their start and end apart: 5 -> 5, of which waited for: 1 -> 1; matrix products, arithmetic and copies ran while one was open for 0% -> 0% of each run, Pallas kernels for 45% -> 44%
where the time goes in v2:
time: 40.4 us; the launch traced here: 40 us
  Pallas kernels  24.5 us (61%)
  starting transfers between devices  12.6 us (31%)
  waiting for transfers between devices  1.79 us (4%)
  local copies, waits for them, and re-layouts  0.78 us (2%)
    all_to_all x2, starting transfers between devices, exchange(): lax.all_to_all(blocks, 'seq', 0, 0, axis_index_groups=teams, tiled=True)  9.57 us
    pallas_call x1, Pallas kernels, shards(): pl.pallas_call(local_kernel, out_shape=shape(tiled, F32), in_specs=[hbm]...  8.75 us
    pallas_call x1, Pallas kernels, shards(): pl.pallas_call(functools.partial(near_kernel, wide), out_shape=shape((12...  7.19 us
    pallas_call x1, Pallas kernels, shards(): pl.pallas_call(functools.partial(prep_kernel, wide), out_shape=(shape((ne...  3.82 us
    ppermute x3, starting transfers between devices, from_partner(): return lax.ppermute(block, axis, [(i, i ^ flip) for i in range(count)])  3.04 us
    pallas_call x1, Pallas kernels, shards(): pl.pallas_call(functools.partial(merge_kernel, wide), out_shape=shape((ro...  2.93 us
    pallas_call x1, Pallas kernels, shards(): pl.pallas_call(functools.partial(owned_kernel, wide), out_shape=shape((ba...  1.81 us
    all_to_all x2, waiting for transfers between devices, exchange(): lax.all_to_all(blocks, 'seq', 0, 0, axis_index_groups=teams, tiled=True)  1.78 us
  transfers between devices with their start and end apart: 5, of which 1 were waited for; matrix products, arithmetic and copies ran while one was open for 0% of the time, Pallas kernels for 44%

profile of v2, /device:TPU:0, one launch (start us, length us, event | category | flops | bytes accessed | tf_op | source)
XLA Modules:
  0.0 40.0 jit_solution(5253962182740156263)
XLA Ops:
  0.0 3.8 %prep.1 = (bf16[128,768]{1,0:T(8,128)(2,1)}, bf16[256,768]{1,0:T(8,128)(2,1)}, bf16[16,72,128]{2,1,0:T(8,128)(2,1)}) custom-call(s32[3,16]{1,0:T(4,128)} %offsets_ref.5, bf16[512,768]{1,0:T(8,128)(2,1)} %q_ref.3, bf16[512,768]{1,0:T(8,128)(2,1)} %k_ref.3, bf16[512,768]{1,0:T(8,128)(2,1)} %v_ref.3), custom_call_target="tpu_custom_call" | custom-call | flops 2359296 | bytes 3932160 | tf_op jit(solution)/shard_map/prep/pallas_call | solution.py:515
  3.8 3.0 %collective-permute-start.1 = (bf16[256,768]{1,0:T(8,128)(2,1)}, bf16[256,768]{1,0:T(8,128)(2,1)S(1)}, u32[]{:S(2)}, u32[]{:S(2)}) collective-permute-start(bf16[256,768]{1,0:T(8,128)(2,1)} %get-tuple-element.14.refs_0_), channel_id=1, source_target_pairs={{0,2},{1,3},{2,0},{3,1},{4,6},{5,7},{6,4},{7,5},{8,10},{9,11},{10,... | collective-permute-start | bytes 1179656 | tf_op jit(solution)/shard_map/ppermute | solution.py:35
  6.9 0.0 collective-permute-start
  6.9 5.1 %all-to-all-start = ((bf16[16,72,128]{2,1,0:T(8,128)(2,1)}), bf16[16,72,128]{2,1,0:T(8,128)(2,1)S(1)}, u32[]{:S(2)}, u32[]{:S(2)}) async-start(bf16[16,72,128]{2,1,0:T(8,128)(2,1)} %get-tuple-element.15), calls=%async_computation | async-start | bytes 589824 | tf_op jit(solution)/shard_map/all_to_all | solution.py:496
  12.0 8.8 %local.1.refs_4_ = f32[2,6,512,128]{3,2,1,0:T(8,128)} custom-call(bf16[512,768]{1,0:T(8,128)(2,1)} %q_ref.3, bf16[512,768]{1,0:T(8,128)(2,1)} %k_ref.3, bf16[512,768]{1,0:T(8,128)(2,1)} %v_ref.3), custom_call_target="tpu_custom_call" | custom-call | flops 17179869184 | bytes 5505024 | tf_op jit(solution)/shard_map/local/pallas_call | solution.py:543
  20.7 0.0 copy-start
  20.7 0.0 collective-permute-done.1.refs_2_
  20.8 0.0 copy-start.1
  20.8 1.8 %all-to-all-done.recv_ref = bf16[16,72,128]{2,1,0:T(8,128)(2,1)S(1)} async-done(((bf16[16,72,128]{2,1,0:T(8,128)(2,1)}), bf16[16,72,128]{2,1,0:T(8,128)(2,1)S(1)}, u32[]{:S(2)}, u32[]{:S(2)}) %all-to-all-start) | async-done | bytes 294944 | tf_op jit(solution)/shard_map/all_to_all | solution.py:496
  22.5 0.0 collective-permute-start.2
  22.5 1.8 %owned.1 = bf16[512,128]{1,0:T(8,128)(2,1)} custom-call(bf16[16,72,128]{2,1,0:T(8,128)(2,1)S(1)} %all-to-all-done.recv_ref), custom_call_target="tpu_custom_call" | custom-call | flops 536870912 | bytes 1572864 | tf_op jit(solution)/shard_map/owned/pallas_call | solution.py:556
  24.4 4.5 %all-to-all-start.1 = ((bf16[16,32,128]{2,1,0:T(8,128)(2,1)}), bf16[16,32,128]{2,1,0:T(8,128)(2,1)S(1)}, u32[]{:S(2)}, u32[]{:S(2)}) async-start(bf16[16,32,128]{2,1,0:T(8,128)(2,1)} %bitcast), calls=%async_computation.1 | async-start | bytes 262144 | tf_op jit(solution)/shard_map/all_to_all | solution.py:496
  28.8 0.0 collective-permute-done.refs_1_
  28.9 0.0 collective-permute-done.2.refs_3_
  28.9 0.0 copy-start.2
  28.9 0.8 %copy-done.2 = bf16[256,768]{1,0:T(8,128)(2,1)} copy-done((bf16[256,768]{1,0:T(8,128)(2,1)}, bf16[256,768]{1,0:T(8,128)(2,1)S(1)}, u32[]{:S(2)}) %copy-start.2) | copy-done | bytes 393240
  29.6 0.0 copy-done.1
  29.6 7.2 %near.1.state_ref = f32[72,512,128]{2,1,0:T(8,128)} custom-call(s32[3,16]{1,0:T(4,128)} %offsets_ref.5, bf16[128,768]{1,0:T(8,128)(2,1)} %get-tuple-element.13.q_ref, bf16[256,768]{1,0:T(8,128)(2,1)} %get-tuple-element.14.refs_0_, bf16[256,768]{1,0:T(8,128)(2,1)} %collective-permute-done.refs_1_, bf16[256,768]{1,0:T(8,128)(2,1)} %copy-done.1, ...), custom_call_target="tpu_custom_call" | custom-call | flops 1073741824 | bytes 3145728 | tf_op jit(solution)/shard_map/near/pallas_call | solution.py:571
  36.8 0.0 all-to-all-done.1
  36.9 0.0 copy-done
  36.9 2.9 %merge.1 = bf16[512,768]{1,0:T(8,128)(2,1)} custom-call(s32[3,16]{1,0:T(4,128)S(1)} %copy-done, bf16[512,128]{1,0:T(8,128)(2,1)S(1)} %bitcast.2, f32[72,512,128]{2,1,0:T(8,128)} %near.1.state_ref), custom_call_target="tpu_custom_call" | custom-call | flops 402653184 | bytes 5505024 | tf_op jit(solution)/shard_map/merge/pallas_call | solution.py:591
Async XLA Ops:
  3.8 16.9 %collective-permute-start.1 = (bf16[256,768]{1,0:T(8,128)(2,1)}, bf16[256,768]{1,0:T(8,128)(2,1)S(1)}, u32[]{:S(2)}, u32[]{:S(2)}) collective-permute-start(bf16[256,768]{1,0:T(8,128)(2,1)} %get-tuple-element.14.refs_0_), channel_id=1, source_target_pairs={{0,2},{1,3},{2,0},{3,1},{4,6},{5,7},{6,4},{7,5},{8,10},{9,11},{10,... | collective-permute-start | bytes 1179656 | tf_op jit(solution)/shard_map/ppermute | solution.py:35
  6.9 22.0 %collective-permute-start = (bf16[256,768]{1,0:T(8,128)(2,1)}, bf16[256,768]{1,0:T(8,128)(2,1)}, u32[]{:S(2)}, u32[]{:S(2)}) collective-permute-start(bf16[256,768]{1,0:T(8,128)(2,1)} %get-tuple-element.14.refs_0_), channel_id=1, source_target_pairs={{0,1},{1,0},{2,3},{3,2},{4,5},{5,4},{6,7},{7,6},{8,9},{9,8},{10,11... | collective-permute-start | bytes 1179656 | tf_op jit(solution)/shard_map/ppermute | solution.py:35
  6.9 15.7 %all-to-all-start = ((bf16[16,72,128]{2,1,0:T(8,128)(2,1)}), bf16[16,72,128]{2,1,0:T(8,128)(2,1)S(1)}, u32[]{:S(2)}, u32[]{:S(2)}) async-start(bf16[16,72,128]{2,1,0:T(8,128)(2,1)} %get-tuple-element.15), calls=%async_computation | async-start | bytes 589824 | tf_op jit(solution)/shard_map/all_to_all | solution.py:496
  20.7 16.1 %copy-start = (s32[3,16]{1,0:T(4,128)S(1)}, s32[3,16]{1,0:T(4,128)}, u32[]{:S(2)}) copy-start(s32[3,16]{1,0:T(4,128)} %offsets_ref.5) | copy-start | bytes 580
  20.8 8.9 %copy-start.1 = (bf16[256,768]{1,0:T(8,128)(2,1)}, bf16[256,768]{1,0:T(8,128)(2,1)S(1)}, u32[]{:S(2)}) copy-start(bf16[256,768]{1,0:T(8,128)(2,1)S(1)} %collective-permute-done.1.refs_2_) | copy-start | bytes 1179652
  22.5 6.3 %collective-permute-start.2 = (bf16[256,768]{1,0:T(8,128)(2,1)S(1)}, bf16[256,768]{1,0:T(8,128)(2,1)S(1)}, u32[]{:S(2)}, u32[]{:S(2)}) collective-permute-start(bf16[256,768]{1,0:T(8,128)(2,1)S(1)} %collective-permute-done.1.refs_2_), channel_id=1, source_target_pairs={{0,1},{1,0},{2,3},{3,2},{4,5},{5,4},{6,7},{7,6},{8,9},{9,8},{10,11... | collective-permute-start | bytes 1179656 | tf_op jit(solution)/shard_map/ppermute | solution.py:35
  24.4 12.5 %all-to-all-start.1 = ((bf16[16,32,128]{2,1,0:T(8,128)(2,1)}), bf16[16,32,128]{2,1,0:T(8,128)(2,1)S(1)}, u32[]{:S(2)}, u32[]{:S(2)}) async-start(bf16[16,32,128]{2,1,0:T(8,128)(2,1)} %bitcast), calls=%async_computation.1 | async-start | bytes 262144 | tf_op jit(solution)/shard_map/all_to_all | solution.py:496
  28.9 0.8 %copy-start.2 = (bf16[256,768]{1,0:T(8,128)(2,1)}, bf16[256,768]{1,0:T(8,128)(2,1)S(1)}, u32[]{:S(2)}) copy-start(bf16[256,768]{1,0:T(8,128)(2,1)S(1)} %collective-permute-done.2.refs_3_) | copy-start | bytes 1179652

commit v3 on v2

--- a/solution.py
+++ b/solution.py
@@ -288,8 +288,8 @@
 
 
 def near_kernel(wide, offsets_ref, q_ref, *refs):
-    kv_refs, (own_ref, state_out) = refs[:NEAR_SPAN], refs[NEAR_SPAN : NEAR_SPAN + 2]
-    q_stage, kv_stage, own, picked, kv_sems, own_sems, out_sems = refs[NEAR_SPAN + 2 :]
+    kv_refs, (own_ref, base_out, picked_out) = refs[:NEAR_SPAN], refs[NEAR_SPAN : NEAR_SPAN + 3]
+    q_stage, kv_stage, own, base, picked, kv_sems, own_sems, out_sems = refs[NEAR_SPAN + 3 :]
     near_rows = q_ref.shape[0]
     rows = own_ref.shape[2]
     groups = rows // MID_SPAN
@@ -335,11 +335,12 @@
                         own[0, t, every(o, chunk), :] = branch[o]
                 for s in range(wide):
                     for kind, blocks in enumerate((branch, lse)):
-                        base = (2 * s + kind) * groups + chunk * 8
-                        picked[t, base : base + 8] = pick(blocks, wide_bits[s])
+                        at = (2 * s + kind) * groups + chunk * 8
+                        picked[t, at : at + 8] = pick(blocks, wide_bits[s])
+            base[t] = own[0, t].astype(BF)
         tiles = range(part * PART_TILES, (part + 1) * PART_TILES)
-        pairs = [(own.at[0, t], state_out.at[t]) for t in tiles]
-        pairs += [(picked.at[t], state_out.at[D // TILE + t, : 2 * wide * groups]) for t in tiles]
+        pairs = [(base.at[t], base_out.at[t]) for t in tiles]
+        pairs += [(picked.at[t], picked_out.at[t]) for t in tiles]
         leaving += flights(pairs, out_sems.at[part])
     for copy in leaving:
         copy.wait()
@@ -398,12 +399,12 @@
         copy.wait()
 
 
-def merge_kernel(wide, offsets_ref, back_ref, state_ref, out_ref, base, picked, out, in_sems, out_sems):
+def merge_kernel(wide, offsets_ref, back_ref, base_ref, picked_ref, out_ref, base, picked, out, in_sems, out_sems):
     rows = out_ref.shape[0]
     groups = rows // MID_SPAN
     arrivals = [
         flights(
-            [(state_ref.at[D // TILE + t, : 2 * wide * groups], picked.at[t]), (state_ref.at[t], base.at[t])], in_sems.at[t]
+            [(picked_ref.at[t], picked.at[t]), (base_ref.at[t], base.at[t])], in_sems.at[t]
         )
         for t in range(D // TILE)
     ]
@@ -449,7 +450,7 @@
         hits = [row_in_16 == off for off in offs]
         arrivals[t][1].wait()
         for g in range(groups):
-            block = base[t, g * MID_SPAN : (g + 1) * MID_SPAN]
+            block = base[t, g * MID_SPAN : (g + 1) * MID_SPAN].astype(F32)
             for hit, (branch, _) in zip(hits, results):
                 block = jnp.where(hit, jnp.broadcast_to(branch[g : g + 1], (MID_SPAN, TILE)), block)
             out[g * MID_SPAN : (g + 1) * MID_SPAN, lanes] = block.astype(BF)
@@ -568,15 +569,19 @@
     if wide == 1:
         far_branch, far_lse = far_by_gather(queries, key_rows, value_rows, offsets[2], count)
         own = jnp.stack(combine(own[0], own[1], far_branch, far_lse))
-    state = pl.pallas_call(
+    base, picked = pl.pallas_call(
         functools.partial(near_kernel, wide),
-        out_shape=shape((12 * D // TILE, rows, TILE), F32),
+        out_shape=(
+            shape((24 * D // TILE, rows, TILE), BF),
+            shape((48 * D // TILE, 2 * wide * groups, TILE), F32),
+        ),
         in_specs=[smem] + [hbm] * (2 + NEAR_SPAN),
-        out_specs=hbm,
+        out_specs=(hbm, hbm),
         scratch_shapes=[
             pltpu.VMEM((near_rows, D), BF),
             pltpu.VMEM((2, NEAR_SPAN * near_rows, D), BF),
             pltpu.VMEM(tiled, F32),
+            pltpu.VMEM((D // TILE, rows, TILE), BF),
             pltpu.VMEM((D // TILE, 2 * wide * groups, TILE), F32),
             sems(PARTS, 1 + 2 * NEAR_SPAN),
             sems(PARTS, 2 * PART_TILES),
@@ -586,15 +591,15 @@
         cost_estimate=cost(4 * near_rows * rows * H * 256, 8 * rows * D, near_rows * rows * H),
         name="near",
     )(offsets, near_q, near_kv, near_core, near_side, near_both, own)
-    state, back = lax.optimization_barrier((state, back))
+    base, picked, back = lax.optimization_barrier((base, picked, back))
 
     return pl.pallas_call(
         functools.partial(merge_kernel, wide),
         out_shape=shape((rows, D), BF),
-        in_specs=[smem, vmem, hbm],
+        in_specs=[smem, vmem, hbm, hbm],
         out_specs=hbm,
         scratch_shapes=[
-            pltpu.VMEM((D // TILE, rows, TILE), F32),
+            pltpu.VMEM((D // TILE, rows, TILE), BF),
             pltpu.VMEM((D // TILE, 2 * wide * groups, TILE), F32),
             pltpu.VMEM((rows, D), BF),
             sems(D // TILE, 2),
@@ -603,7 +608,7 @@
         compiler_params=params(SMALL_BYTES),
         cost_estimate=cost(2 * rows * rows * D, 14 * rows * D),
         name="merge",
-    )(offsets, back, state)
+    )(offsets, back, base, picked)
 
 
 def solution(mesh):

time: 40.4 us -> 40.2 us (level)
  transfers between devices with their start and end apart: 5 -> 5, of which waited for: 1 -> 2; matrix products, arithmetic and copies ran while one was open for 0% -> 0% of each run, Pallas kernels for 44% -> 44%
where the time goes in v3:
time: 40.2 us; the launch traced here: 39.8 us
  Pallas kernels  24.3 us (60%)
  starting transfers between devices  12.6 us (31%)
  waiting for transfers between devices  1.96 us (5%)
  local copies, waits for them, and re-layouts  0.77 us (2%)
    all_to_all x2, starting transfers between devices, exchange(): lax.all_to_all(blocks, 'seq', 0, 0, axis_index_groups=teams, tiled=True)  9.54 us
    pallas_call x1, Pallas kernels, shards(): pl.pallas_call(local_kernel, out_shape=shape(tiled, F32), in_specs=[hbm]...  8.72 us
    pallas_call x1, Pallas kernels, shards(): pl.pallas_call(functools.partial(near_kernel, wide), out_shape=(shape((24...  7 us
    pallas_call x1, Pallas kernels, shards(): pl.pallas_call(functools.partial(prep_kernel, wide), out_shape=(shape((ne...  3.82 us
    ppermute x3, starting transfers between devices, from_partner(): return lax.ppermute(block, axis, [(i, i ^ flip) for i in range(count)])  3.04 us
    pallas_call x1, Pallas kernels, shards(): pl.pallas_call(functools.partial(merge_kernel, wide), out_shape=shape((ro...  2.93 us
    all_to_all x2, waiting for transfers between devices, exchange(): lax.all_to_all(blocks, 'seq', 0, 0, axis_index_groups=teams, tiled=True)  1.95 us
    pallas_call x1, Pallas kernels, shards(): pl.pallas_call(functools.partial(owned_kernel, wide), out_shape=shape((ba...  1.81 us
  transfers between devices with their start and end apart: 5, of which 2 were waited for; matrix products, arithmetic and copies ran while one was open for 0% of the time, Pallas kernels for 44%

profile of v3, /device:TPU:0, one launch (start us, length us, event | category | flops | bytes accessed | tf_op | source)
XLA Modules:
  0.0 39.8 jit_solution(9738022396008573037)
XLA Ops:
  0.0 3.8 %prep.1 = (bf16[128,768]{1,0:T(8,128)(2,1)}, bf16[256,768]{1,0:T(8,128)(2,1)}, bf16[16,72,128]{2,1,0:T(8,128)(2,1)}) custom-call(s32[3,16]{1,0:T(4,128)} %offsets_ref.5, bf16[512,768]{1,0:T(8,128)(2,1)} %q_ref.3, bf16[512,768]{1,0:T(8,128)(2,1)} %k_ref.3, bf16[512,768]{1,0:T(8,128)(2,1)} %v_ref.3), custom_call_target="tpu_custom_call" | custom-call | flops 2359296 | bytes 3932160 | tf_op jit(solution)/shard_map/prep/pallas_call | solution.py:516
  3.8 3.0 %collective-permute-start.1 = (bf16[256,768]{1,0:T(8,128)(2,1)}, bf16[256,768]{1,0:T(8,128)(2,1)S(1)}, u32[]{:S(2)}, u32[]{:S(2)}) collective-permute-start(bf16[256,768]{1,0:T(8,128)(2,1)} %get-tuple-element.17.refs_0_), channel_id=1, source_target_pairs={{0,2},{1,3},{2,0},{3,1},{4,6},{5,7},{6,4},{7,5},{8,10},{9,11},{10,... | collective-permute-start | bytes 1179656 | tf_op jit(solution)/shard_map/ppermute | solution.py:35
  6.9 0.0 collective-permute-start
  6.9 5.1 %all-to-all-start = ((bf16[16,72,128]{2,1,0:T(8,128)(2,1)}), bf16[16,72,128]{2,1,0:T(8,128)(2,1)S(1)}, u32[]{:S(2)}, u32[]{:S(2)}) async-start(bf16[16,72,128]{2,1,0:T(8,128)(2,1)} %get-tuple-element.18), calls=%async_computation | async-start | bytes 589824 | tf_op jit(solution)/shard_map/all_to_all | solution.py:497
  12.0 0.0 copy-start
  12.0 8.7 %local.1.refs_4_ = f32[2,6,512,128]{3,2,1,0:T(8,128)} custom-call(bf16[512,768]{1,0:T(8,128)(2,1)} %q_ref.3, bf16[512,768]{1,0:T(8,128)(2,1)} %k_ref.3, bf16[512,768]{1,0:T(8,128)(2,1)} %v_ref.3), custom_call_target="tpu_custom_call" | custom-call | flops 17179869184 | bytes 5505024 | tf_op jit(solution)/shard_map/local/pallas_call | solution.py:544
  20.7 0.0 collective-permute-done.1.refs_2_
  20.7 0.0 copy-start.1
  20.7 1.8 %all-to-all-done.recv_ref = bf16[16,72,128]{2,1,0:T(8,128)(2,1)S(1)} async-done(((bf16[16,72,128]{2,1,0:T(8,128)(2,1)}), bf16[16,72,128]{2,1,0:T(8,128)(2,1)S(1)}, u32[]{:S(2)}, u32[]{:S(2)}) %all-to-all-start) | async-done | bytes 294944 | tf_op jit(solution)/shard_map/all_to_all | solution.py:497
  22.5 0.0 collective-permute-start.2
  22.5 1.8 %owned.1 = bf16[512,128]{1,0:T(8,128)(2,1)} custom-call(bf16[16,72,128]{2,1,0:T(8,128)(2,1)S(1)} %all-to-all-done.recv_ref), custom_call_target="tpu_custom_call" | custom-call | flops 536870912 | bytes 1572864 | tf_op jit(solution)/shard_map/owned/pallas_call | solution.py:557
  24.4 4.4 %all-to-all-start.1 = ((bf16[16,32,128]{2,1,0:T(8,128)(2,1)}), bf16[16,32,128]{2,1,0:T(8,128)(2,1)S(1)}, u32[]{:S(2)}, u32[]{:S(2)}) async-start(bf16[16,32,128]{2,1,0:T(8,128)(2,1)} %bitcast), calls=%async_computation.1 | async-start | bytes 262144 | tf_op jit(solution)/shard_map/all_to_all | solution.py:497
  28.8 0.0 collective-permute-done.refs_1_
  28.8 0.0 collective-permute-done.2.refs_3_
  28.8 0.0 copy-start.2
  28.8 0.8 %copy-done.2 = bf16[256,768]{1,0:T(8,128)(2,1)} copy-done((bf16[256,768]{1,0:T(8,128)(2,1)}, bf16[256,768]{1,0:T(8,128)(2,1)S(1)}, u32[]{:S(2)}) %copy-start.2) | copy-done | bytes 393240
  29.6 0.0 copy-done.1
  29.6 7.0 %near.1 = (bf16[144,512,128]{2,1,0:T(8,128)(2,1)}, f32[288,128,128]{2,1,0:T(8,128)}) custom-call(s32[3,16]{1,0:T(4,128)} %offsets_ref.5, bf16[128,768]{1,0:T(8,128)(2,1)} %get-tuple-element.16.q_ref, bf16[256,768]{1,0:T(8,128)(2,1)} %get-tuple-element.17.refs_0_, bf16[256,768]{1,0:T(8,128)(2,1)} %collective-permute-done.refs_1_, bf16[256,768]{1,0:T(8,128)(2,1)} %copy-done.1, ...), custom_call_target="tpu_custom_call" | custom-call | flops 1073741824 | bytes 3145728 | tf_op jit(solution)/shard_map/near/pallas_call | solution.py:572
  36.6 0.1 all-to-all-done.1
  36.7 0.0 copy-done
  36.7 2.9 %merge.1 = bf16[512,768]{1,0:T(8,128)(2,1)} custom-call(s32[3,16]{1,0:T(4,128)S(1)} %copy-done, bf16[512,128]{1,0:T(8,128)(2,1)S(1)} %bitcast.2, bf16[144,512,128]{2,1,0:T(8,128)(2,1)} %get-tuple-element.25.base_ref, f32[288,128,128]{2,1,0:T(8,128)} %get-tuple-element.26.picked_ref), custom_call_target="tpu_custom_call" | custom-call | flops 402653184 | bytes 5505024 | tf_op jit(solution)/shard_map/merge/pallas_call | solution.py:596
Async XLA Ops:
  3.8 16.9 %collective-permute-start.1 = (bf16[256,768]{1,0:T(8,128)(2,1)}, bf16[256,768]{1,0:T(8,128)(2,1)S(1)}, u32[]{:S(2)}, u32[]{:S(2)}) collective-permute-start(bf16[256,768]{1,0:T(8,128)(2,1)} %get-tuple-element.17.refs_0_), channel_id=1, source_target_pairs={{0,2},{1,3},{2,0},{3,1},{4,6},{5,7},{6,4},{7,5},{8,10},{9,11},{10,... | collective-permute-start | bytes 1179656 | tf_op jit(solution)/shard_map/ppermute | solution.py:35
  6.9 22.0 %collective-permute-start = (bf16[256,768]{1,0:T(8,128)(2,1)}, bf16[256,768]{1,0:T(8,128)(2,1)}, u32[]{:S(2)}, u32[]{:S(2)}) collective-permute-start(bf16[256,768]{1,0:T(8,128)(2,1)} %get-tuple-element.17.refs_0_), channel_id=1, source_target_pairs={{0,1},{1,0},{2,3},{3,2},{4,5},{5,4},{6,7},{7,6},{8,9},{9,8},{10,11... | collective-permute-start | bytes 1179656 | tf_op jit(solution)/shard_map/ppermute | solution.py:35
  6.9 15.7 %all-to-all-start = ((bf16[16,72,128]{2,1,0:T(8,128)(2,1)}), bf16[16,72,128]{2,1,0:T(8,128)(2,1)S(1)}, u32[]{:S(2)}, u32[]{:S(2)}) async-start(bf16[16,72,128]{2,1,0:T(8,128)(2,1)} %get-tuple-element.18), calls=%async_computation | async-start | bytes 589824 | tf_op jit(solution)/shard_map/all_to_all | solution.py:497
  12.0 24.8 %copy-start = (s32[3,16]{1,0:T(4,128)S(1)}, s32[3,16]{1,0:T(4,128)}, u32[]{:S(2)}) copy-start(s32[3,16]{1,0:T(4,128)} %offsets_ref.5) | copy-start | bytes 580
  20.7 8.9 %copy-start.1 = (bf16[256,768]{1,0:T(8,128)(2,1)}, bf16[256,768]{1,0:T(8,128)(2,1)S(1)}, u32[]{:S(2)}) copy-start(bf16[256,768]{1,0:T(8,128)(2,1)S(1)} %collective-permute-done.1.refs_2_) | copy-start | bytes 1179652
  22.5 6.3 %collective-permute-start.2 = (bf16[256,768]{1,0:T(8,128)(2,1)S(1)}, bf16[256,768]{1,0:T(8,128)(2,1)S(1)}, u32[]{:S(2)}, u32[]{:S(2)}) collective-permute-start(bf16[256,768]{1,0:T(8,128)(2,1)S(1)} %collective-permute-done.1.refs_2_), channel_id=1, source_target_pairs={{0,1},{1,0},{2,3},{3,2},{4,5},{5,4},{6,7},{7,6},{8,9},{9,8},{10,11... | collective-permute-start | bytes 1179656 | tf_op jit(solution)/shard_map/ppermute | solution.py:35
  24.4 12.4 %all-to-all-start.1 = ((bf16[16,32,128]{2,1,0:T(8,128)(2,1)}), bf16[16,32,128]{2,1,0:T(8,128)(2,1)S(1)}, u32[]{:S(2)}, u32[]{:S(2)}) async-start(bf16[16,32,128]{2,1,0:T(8,128)(2,1)} %bitcast), calls=%async_computation.1 | async-start | bytes 262144 | tf_op jit(solution)/shard_map/all_to_all | solution.py:497
  28.8 0.8 %copy-start.2 = (bf16[256,768]{1,0:T(8,128)(2,1)}, bf16[256,768]{1,0:T(8,128)(2,1)S(1)}, u32[]{:S(2)}) copy-start(bf16[256,768]{1,0:T(8,128)(2,1)S(1)} %collective-permute-done.2.refs_3_) | copy-start | bytes 1179652
